TPU v7x, 128 devices: a whole 4x4x4 slice. The times are simulated.
128 devices in a mesh: shot: 16 (over z_hi, x, core), slab: 8 (over y, z_lo).
Axes of the slice: x: 4, y: 4, z: 4 (z_hi: 2, z_lo: 2; z = z_hi * 2 + z_lo), core: 2. Of those that a mesh axis runs over, the one named last changes fastest.
Arguments:
- kappa: float32 [128, 256, 256], P('slab', 'shot'), may hold values from 0.05 to 0.25
- buoyancy: float32 [128, 256, 256], P('slab', 'shot'), may hold values from 0.5 to 1
- anchors: int32 [16, 2], replicated, may hold values from 0 to 128
- wave_start: float32 [16, 2, 128, 128, 128], P('shot', None, 'slab'), may hold values from -1.8 to 1.8
- adjoint_start: float32 [16, 2, 128, 128, 128], P('shot', None, 'slab'), may hold values from -1.8 to 1.8
- wavelet: float32 [16, 4], P('shot'), may hold values from -4 to 4
- source_cell: int32 [16, 3], P('shot'), may hold values from 0 to 127
- receiver_cells: int32 [16, 512, 3], P('shot'), may hold values from 0 to 127
- observed: float32 [16, 4, 512], P('shot'), may hold values from -3 to 3
Outputs:
- model_grad: float32 [128, 256, 256], P('slab', 'shot')
- wave_end: float32 [16, 2, 128, 128, 128], P('shot', None, 'slab')
- adjoint_end: float32 [16, 2, 128, 128, 128], P('shot', None, 'slab')
Inputs may be any that keep to these rules, and one draw needn't show every extreme that they name: `anchors`: apertures lie inside the model; several shots' apertures may cover the same cells. `receiver_cells`: several receivers may share a cell.
All inputs are finite; a program needn't handle non-finite values.
Results may differ from a plain program's by a relative error of at most 0.00002.
Values sent between devices are 32-bit elements; how exact they have to be, the bound alone decides.
A program may use at most 128 MiB of HBM per device.

v0:
```python
import jax
import jax.numpy as jnp
from jax import lax
from jax.sharding import PartitionSpec as P

NT = 4


def with_halo(array, sides, width):
    for axis, dim in sides:
        count, length = (lax.axis_size(axis), array.shape[dim])
        up = [(i, (i + 1) % count) for i in range(count - 1)]
        down = [(j, i) for i, j in up]
        last = lax.slice_in_dim(array, length - width, length, axis=dim)
        first = lax.slice_in_dim(array, 0, width, axis=dim)
        before = lax.ppermute(last, axis, up)
        after = lax.ppermute(first, axis, down)
        array = jnp.concatenate([before, array, after], axis=dim)
    return array


def spread_of(field, faces):
    depth_face, row_face, col_face = faces
    pad_depth = with_halo(field, (("slab", 0),), 1)
    flux = depth_face * (pad_depth[1:] - pad_depth[:-1])
    result = flux[1:] - flux[:-1]
    pad_rows = jnp.pad(field, ((0, 0), (1, 1), (0, 0)))
    flux = row_face * (pad_rows[:, 1:] - pad_rows[:, :-1])
    result = result + (flux[:, 1:] - flux[:, :-1])
    pad_cols = jnp.pad(field, ((0, 0), (0, 0), (1, 1)))
    flux = col_face * (pad_cols[:, :, 1:] - pad_cols[:, :, :-1])
    return result + (flux[:, :, 1:] - flux[:, :, :-1])


def add_cells(field, positions, amounts):
    shape = field.shape
    return field.reshape(-1).at[positions].add(amounts).reshape(shape)


def shards(
    kappa,
    buoyancy,
    anchors,
    wave_start,
    adjoint_start,
    wavelet,
    source_cell,
    receiver_cells,
    observed,
):
    depth_cells = kappa.shape[0]
    own_rows = kappa.shape[1]
    model_side = kappa.shape[2]
    aperture = wave_start.shape[3]
    groups = lax.axis_size("shot")
    shot_index = lax.axis_index("shot")
    anchor = anchors[shot_index]
    row_anchor = anchor[0]
    col_anchor = anchor[1]
    stacked = jnp.stack([kappa, buoyancy])
    gathered = lax.all_gather(stacked, "shot", axis=2, tiled=True)
    window = lax.dynamic_slice(
        gathered,
        (row_anchor * 0, row_anchor * 0, row_anchor, col_anchor),
        (2, depth_cells, aperture, aperture),
    )
    kappa_window = window[0]
    buoy_window = window[1]
    padded_buoy = with_halo(buoy_window, (("slab", 0),), 1)
    depth_face = 0.5 * (padded_buoy[1:] + padded_buoy[:-1])
    pad_rows = jnp.pad(buoy_window, ((0, 0), (1, 1), (0, 0)))
    pad_cols = jnp.pad(buoy_window, ((0, 0), (0, 0), (1, 1)))
    row_face = 0.5 * (pad_rows[:, 1:] + pad_rows[:, :-1])
    col_face = 0.5 * (pad_cols[:, :, 1:] + pad_cols[:, :, :-1])
    faces = (depth_face, row_face, col_face)
    depth_start = lax.axis_index("slab") * depth_cells
    receivers = receiver_cells[0]
    local_depth = receivers[:, 0] - depth_start
    receiver_valid = (local_depth >= 0) & (local_depth < depth_cells)
    receiver_flat = (
        jnp.clip(local_depth, 0, depth_cells - 1) * aperture + receivers[:, 1]
    ) * aperture + receivers[:, 2]
    source = source_cell[0]
    source_depth = source[0] - depth_start
    source_valid = (source_depth >= 0) & (source_depth < depth_cells)
    source_flat = (
        jnp.clip(source_depth, 0, depth_cells - 1) * aperture + source[1]
    ) * aperture + source[2]
    before = wave_start[0, 0]
    current = wave_start[0, 1]
    spreads = []
    residuals = []
    for moment in range(NT):
        spread = spread_of(current, faces)
        spreads.append(spread)
        following = 2.0 * current - before + kappa_window * spread
        following = add_cells(
            following, source_flat[None], jnp.where(source_valid, wavelet[0, moment], 0.0)[None]
        )
        sampled = following.reshape(-1)[receiver_flat]
        residuals.append(jnp.where(receiver_valid, sampled - observed[0, moment], 0.0))
        before = current
        current = following
    after = adjoint_start[0, 0]
    later = adjoint_start[0, 1]
    imaging = None
    for moment in reversed(range(NT)):
        adjoint_now = 2.0 * later - after + spread_of(kappa_window * later, faces)
        adjoint_now = add_cells(adjoint_now, receiver_flat, residuals[moment])
        term = adjoint_now * spreads[moment]
        imaging = term if imaging is None else imaging + term
        after = later
        later = adjoint_now
    embedded = lax.dynamic_update_slice(
        jnp.zeros((depth_cells, own_rows * groups, model_side), jnp.float32),
        imaging,
        (row_anchor * 0, row_anchor, col_anchor),
    )
    gradient_rows = lax.psum_scatter(embedded, "shot", scatter_dimension=1, tiled=True)
    return (gradient_rows, jnp.stack([before, current])[None], jnp.stack([after, later])[None])


def solution(mesh):
    in_specs = (
        P("slab", "shot", None),
        P("slab", "shot", None),
        P(),
        P("shot", None, "slab", None, None),
        P("shot", None, "slab", None, None),
        P("shot", None),
        P("shot", None),
        P("shot", None, None),
        P("shot", None, None),
    )
    out_specs = (
        P("slab", "shot", None),
        P("shot", None, "slab", None, None),
        P("shot", None, "slab", None, None),
    )
    return jax.shard_map(shards, mesh=mesh, in_specs=in_specs, out_specs=out_specs, check_vma=False)
```

profile of v0, /device:TPU:0, one launch (start us, length us, event | category | flops | bytes accessed | tf_op | source)
XLA Modules:
  0.0 375.2 jit_solution(16419638537728177638)
XLA Ops:
  29.6 56.8 %all-gather.2.cloned.1.call-done = f32[2,16,256,256]{3,2,1,0:T(8,128)} async-done(((f32[2,16,16,256]{3,2,1,0:T(8,128)}), f32[2,16,256,256]{3,2,1,0:T(8,128)}) %all-gather.2.cloned.1.call-update) | async-done | bytes 8388624 | tf_op jit(solution)/shard_map/all_gather | solution.py:61
  88.9 4.5 %collective-permute-start.1 = (f32[1,128,128]{2,1,0:T(8,128)S(1)}, f32[1,128,128]{2,1,0:T(8,128)S(1)}, u32[]{:S(2)}, u32[]{:S(2)}) collective-permute-start(f32[1,128,128]{2,1,0:T(8,128)S(1)} %get-tuple-element.65), channel_id=1, source_target_pairs={{0,1},{1,2},{2,3},{3,4},{4,5},{5,6},{6,7},{8,9},{9,10},{10,11},{11... | collective-permute-start | bytes 196616 | tf_op jit(solution)/shard_map/ppermute | solution.py:16
  111.2 7.7 %gather_fusion.3 = f32[512]{0:T(512)} fusion(f32[262144]{0:T(1024)} %copy-done.9, s32[1024]{0:T(1024)S(1)} %pad_clamp_fusion), kind=kCustom, calls=%fused_computation.3 | custom fusion | bytes 6144 | tf_op jit(solution)/shard_map/gather | solution.py:100
  121.1 4.8 %multiply_add_fusion.3 = (f32[16,128,128]{2,1,0:T(8,128)S(1)}, f32[16,128,128]{2,1,0:T(8,128)}) fusion(f32[16,128,128]{2,1,0:T(8,128)S(1)} %bitcast.114, f32[2,16,256,256]{3,2,1,0:T(8,128)} %all-gather.2.cloned.1.call-done, s32[]{:T(128)S(6)} %select_n.55, s32[]{:T(128)S(6)} %select_n.56, f32[1,2,16,128,128]{4,3,2,1,0:T(8,128)} %param.20, ...), kind=kLoop, calls=%fused_computation.128 | loop fusion | flops 2359296 | bytes 11534344 | tf_op jit(solution)/shard_map/add | solution.py:96
  126.7 4.5 %collective-permute-start.9 = (f32[1,128,128]{2,1,0:T(8,128)S(1)}, f32[1,128,128]{2,1,0:T(8,128)S(1)}, u32[]{:S(2)}, u32[]{:S(2)}) collective-permute-start(f32[1,128,128]{2,1,0:T(8,128)S(1)} %get-tuple-element.76), channel_id=1, source_target_pairs={{0,1},{1,2},{2,3},{3,4},{4,5},{5,6},{6,7},{8,9},{9,10},{10,11},{11... | collective-permute-start | bytes 196616 | tf_op jit(solution)/shard_map/ppermute | solution.py:16
  135.7 8.0 %gather_fusion.2 = f32[512]{0:T(512)} fusion(f32[262144]{0:T(1024)} %copy-done.12, s32[1024]{0:T(1024)S(1)} %pad_clamp_fusion), kind=kCustom, calls=%fused_computation.2 | custom fusion | bytes 6144 | tf_op jit(solution)/shard_map/gather | solution.py:100
  146.2 4.5 %multiply_add_fusion.2 = (f32[16,128,128]{2,1,0:T(8,128)S(1)}, f32[16,128,128]{2,1,0:T(8,128)}) fusion(f32[16,128,128]{2,1,0:T(8,128)S(1)} %bitcast.115, f32[16,128,128]{2,1,0:T(8,128)S(1)} %bitcast.120, f32[2,16,256,256]{3,2,1,0:T(8,128)} %all-gather.2.cloned.1.call-done, s32[]{:T(128)S(6)} %select_n.55, s32[]{:T(128)S(6)} %select_n.56, ...), kind=kLoop, calls=%fused_computation.127 | loop fusion | flops 2359296 | bytes 11534344 | tf_op jit(solution)/shard_map/add | solution.py:96
  151.5 4.5 %collective-permute-start.11 = (f32[1,128,128]{2,1,0:T(8,128)S(1)}, f32[1,128,128]{2,1,0:T(8,128)S(1)}, u32[]{:S(2)}, u32[]{:S(2)}) collective-permute-start(f32[1,128,128]{2,1,0:T(8,128)S(1)} %get-tuple-element.74), channel_id=1, source_target_pairs={{0,1},{1,2},{2,3},{3,4},{4,5},{5,6},{6,7},{8,9},{9,10},{10,11},{11... | collective-permute-start | bytes 196616 | tf_op jit(solution)/shard_map/ppermute | solution.py:16
  160.7 7.8 %gather_fusion.1 = f32[512]{0:T(512)} fusion(f32[262144]{0:T(1024)} %copy-done.15, s32[1024]{0:T(1024)S(1)} %pad_clamp_fusion), kind=kCustom, calls=%fused_computation.1 | custom fusion | bytes 6144 | tf_op jit(solution)/shard_map/gather | solution.py:100
  171.0 5.4 %multiply_add_fusion.1 = (f32[16,128,128]{2,1,0:T(8,128)}, f32[16,128,128]{2,1,0:T(8,128)}, f32[16,128,128]{2,1,0:T(8,128)S(1)}) fusion(f32[16,128,128]{2,1,0:T(8,128)S(1)} %bitcast.121, f32[16,128,128]{2,1,0:T(8,128)S(1)} %bitcast.126, f32[2,16,256,256]{3,2,1,0:T(8,128)} %all-gather.2.cloned.1.call-done, s32[]{:T(128)S(6)} %select_n.55, s32[]{:T(128)S(6)} %select_n.56, ...), kind=kLoop, calls=%fused_computation.126 | loop fusion | flops 2621440 | bytes 13631496 | tf_op jit(solution)/shard_map/add | solution.py:96
  181.8 6.7 %gather_fusion = f32[512]{0:T(512)S(1)} fusion(f32[262144]{0:T(1024)} %fusion.55, s32[1024]{0:T(1024)S(1)} %pad_clamp_fusion), kind=kCustom, calls=%fused_computation | custom fusion | bytes 6144 | tf_op jit(solution)/shard_map/gather | solution.py:100
  188.6 5.0 %collective-permute-start.3 = (f32[1,128,128]{2,1,0:T(8,128)S(1)}, f32[1,128,128]{2,1,0:T(8,128)S(1)}, u32[]{:S(2)}, u32[]{:S(2)}) collective-permute-start(f32[1,128,128]{2,1,0:T(8,128)S(1)} %get-tuple-element.80), channel_id=1, source_target_pairs={{0,1},{1,2},{2,3},{3,4},{4,5},{5,6},{6,7},{8,9},{9,10},{10,11},{11... | collective-permute-start | bytes 196616 | tf_op jit(solution)/shard_map/ppermute | solution.py:16
  195.5 5.1 %collective-permute-done.2 = f32[1,128,128]{2,1,0:T(8,128)S(1)} collective-permute-done((f32[1,128,128]{2,1,0:T(8,128)S(1)}, f32[1,128,128]{2,1,0:T(8,128)S(1)}, u32[]{:S(2)}, u32[]{:S(2)}) %collective-permute-start.2) | collective-permute-done | bytes 65568 | tf_op jit(solution)/shard_map/ppermute | solution.py:17
  205.5 5.2 %scatter_fusion = f32[262144]{0:T(1024)} fusion(f32[262144]{0:T(1024)} %bitcast.128, s32[512]{0:T(512)S(1)} %bitcast.149, f32[512]{0:T(512)S(1)} %get-tuple-element.91), kind=kCustom, calls=%fused_computation.4 | custom fusion | flops 512 | bytes 8192 | tf_op jit(solution)/shard_map/scatter-add | solution.py:37
  213.7 4.8 %collective-permute-start.13 = (f32[1,128,128]{2,1,0:T(8,128)S(1)}, f32[1,128,128]{2,1,0:T(8,128)S(1)}, u32[]{:S(2)}, u32[]{:S(2)}) collective-permute-start(f32[1,128,128]{2,1,0:T(8,128)S(1)} %get-tuple-element.72), channel_id=1, source_target_pairs={{0,1},{1,2},{2,3},{3,4},{4,5},{5,6},{6,7},{8,9},{9,10},{10,11},{11... | collective-permute-start | bytes 196616 | tf_op jit(solution)/shard_map/ppermute | solution.py:16
  220.4 4.3 %collective-permute-done.12 = f32[1,128,128]{2,1,0:T(8,128)S(1)} collective-permute-done((f32[1,128,128]{2,1,0:T(8,128)S(1)}, f32[1,128,128]{2,1,0:T(8,128)S(1)}, u32[]{:S(2)}, u32[]{:S(2)}) %collective-permute-start.12) | collective-permute-done | bytes 65568 | tf_op jit(solution)/shard_map/ppermute | solution.py:17
  226.4 5.2 %scatter_fusion.1 = f32[262144]{0:T(1024)} fusion(f32[262144]{0:T(1024)} %bitcast.133, s32[512]{0:T(512)S(1)} %bitcast.150, f32[512]{0:T(512)S(1)} %get-tuple-element.90), kind=kCustom, calls=%fused_computation.5 | custom fusion | flops 512 | bytes 8192 | tf_op jit(solution)/shard_map/scatter-add | solution.py:37
  239.2 4.3 %collective-permute-done.14 = f32[1,128,128]{2,1,0:T(8,128)S(1)} collective-permute-done((f32[1,128,128]{2,1,0:T(8,128)S(1)}, f32[1,128,128]{2,1,0:T(8,128)S(1)}, u32[]{:S(2)}, u32[]{:S(2)}) %collective-permute-start.14) | collective-permute-done | bytes 65568 | tf_op jit(solution)/shard_map/ppermute | solution.py:17
  245.2 5.2 %scatter_fusion.2 = f32[262144]{0:T(1024)} fusion(f32[262144]{0:T(1024)} %bitcast.138, s32[512]{0:T(512)S(1)} %bitcast.151, f32[512]{0:T(512)S(1)} %get-tuple-element.89), kind=kCustom, calls=%fused_computation.6 | custom fusion | flops 512 | bytes 8192 | tf_op jit(solution)/shard_map/scatter-add | solution.py:37
  259.0 4.3 %collective-permute-done.16 = f32[1,128,128]{2,1,0:T(8,128)S(1)} collective-permute-done((f32[1,128,128]{2,1,0:T(8,128)S(1)}, f32[1,128,128]{2,1,0:T(8,128)S(1)}, u32[]{:S(2)}, u32[]{:S(2)}) %collective-permute-start.16) | collective-permute-done | bytes 65568 | tf_op jit(solution)/shard_map/ppermute | solution.py:17
  265.1 5.3 %scatter_fusion.3 = f32[262144]{0:T(1024)} fusion(f32[262144]{0:T(1024)} %bitcast.143, s32[512]{0:T(512)S(1)} %bitcast.152, f32[512]{0:T(512)S(1)} %get-tuple-element.88), kind=kCustom, calls=%fused_computation.7 | custom fusion | flops 512 | bytes 8192 | tf_op jit(solution)/shard_map/scatter-add | solution.py:37
  270.4 4.3 %multiply_add_fusion = f32[16,128,128]{2,1,0:T(8,128)} fusion(f32[16,128,128]{2,1,0:T(8,128)} %bitcast.144, f32[16,128,128]{2,1,0:T(8,128)} %get-tuple-element.58, f32[16,128,128]{2,1,0:T(8,128)S(1)} %bitcast.141, f32[16,128,128]{2,1,0:T(8,128)} %get-tuple-element.56, f32[16,128,128]{2,1,0:T(8,128)S(1)} %bitcast.137, f32[16,128,128]{2,1,0:T(8,128)} %get-tuple-element.54, ...), kind=kLoop, calls=%fused_computation.125 | loop fusion | flops 1835008 | bytes 9437184 | tf_op jit(solution)/shard_map/add | solution.py:111
  277.1 13.7 %dynamic_update_slice.3 = f32[16,256,256]{2,1,0:T(8,128)} dynamic-update-slice(f32[16,256,256]{2,1,0:T(8,128)} %broadcast_in_dim.15, f32[16,128,128]{2,1,0:T(8,128)S(1)} %copy-done.33, s32[]{:T(128)} %constant.95.clone.1, s32[]{:T(128)S(6)} %select_n.55, s32[]{:T(128)S(6)} %select_n.56) | dynamic-update-slice | bytes 2097156 | tf_op jit(solution)/shard_map/dynamic_update_slice | solution.py:114
  295.9 72.4 %reduce-scatter.2.cloned.1.call-done = f32[16,16,256]{2,1,0:T(8,128)} async-done(((f32[16,256,256]{2,1,0:T(8,128)}), f32[16,16,256]{2,1,0:T(8,128)}) %reduce-scatter.2.cloned.1.call-update) | async-done | bytes 262160 | tf_op jit(solution)/shard_map/reduce_scatter | solution.py:119
  (179 shorter events, 97.3 us)
Async XLA Ops:
  7.2 17.7 %copy-start.41 = (s32[1,512,3]{1,0,2:T(1,128)S(1)}, s32[1,512,3]{1,0,2:T(1,128)}, u32[]{:S(2)}) copy-start(s32[1,512,3]{1,0,2:T(1,128)} %param.24) | copy-start | bytes 18436
  7.2 19.5 %copy-start.34 = (f32[1,4,512]{2,1,0:T(4,128)S(1)}, f32[1,4,512]{2,1,0:T(4,128)}, u32[]{:S(2)}) copy-start(f32[1,4,512]{2,1,0:T(4,128)} %param.25) | copy-start | bytes 24580
  7.2 79.1 %all-gather.2.cloned.1.call-start = ((), (), s32[]{:S(2)}) async-start(), calls=%async_computation.1 | async-start | bytes 8912896 | tf_op jit(solution)/shard_map/all_gather | solution.py:61
  9.2 359.2 %reduce-scatter.2.cloned.1.call-start = ((), (), s32[]{:S(2)}) async-start(), calls=%async_computation.2 | async-start | bytes 4456448 | tf_op jit(solution)/shard_map/reduce_scatter | solution.py:119
  10.1 86.8 %collective-permute-start.5 = (f32[1,128,128]{2,1,0:T(8,128)S(1)}, f32[1,128,128]{2,1,0:T(8,128)S(1)}, u32[]{:S(2)}, u32[]{:S(2)}) collective-permute-start(f32[1,128,128]{2,1,0:T(8,128)S(1)} %get-tuple-element.66), channel_id=1, source_target_pairs={{0,1},{1,2},{2,3},{3,4},{4,5},{5,6},{6,7},{8,9},{9,10},{10,11},{11... | collective-permute-start | bytes 196616 | tf_op jit(solution)/shard_map/ppermute | solution.py:16
  14.0 82.9 %collective-permute-start.4 = (f32[1,128,128]{2,1,0:T(8,128)S(1)}, f32[1,128,128]{2,1,0:T(8,128)S(1)}, u32[]{:S(2)}, u32[]{:S(2)}) collective-permute-start(f32[1,128,128]{2,1,0:T(8,128)S(1)} %get-tuple-element.67), channel_id=1, source_target_pairs={{1,0},{2,1},{3,2},{4,3},{5,4},{6,5},{7,6},{9,8},{10,9},{11,10},{12... | collective-permute-start | bytes 196616 | tf_op jit(solution)/shard_map/ppermute | solution.py:17
  87.5 9.5 %collective-permute-start = (f32[1,128,128]{2,1,0:T(8,128)S(1)}, f32[1,128,128]{2,1,0:T(8,128)S(1)}, u32[]{:S(2)}, u32[]{:S(2)}) collective-permute-start(f32[1,128,128]{2,1,0:T(8,128)S(1)} %get-tuple-element.64), channel_id=1, source_target_pairs={{1,0},{2,1},{3,2},{4,3},{5,4},{6,5},{7,6},{9,8},{10,9},{11,10},{12... | collective-permute-start | bytes 196616 | tf_op jit(solution)/shard_map/ppermute | solution.py:17
  88.9 8.1 %collective-permute-start.1 = (f32[1,128,128]{2,1,0:T(8,128)S(1)}, f32[1,128,128]{2,1,0:T(8,128)S(1)}, u32[]{:S(2)}, u32[]{:S(2)}) collective-permute-start(f32[1,128,128]{2,1,0:T(8,128)S(1)} %get-tuple-element.65), channel_id=1, source_target_pairs={{0,1},{1,2},{2,3},{3,4},{4,5},{5,6},{6,7},{8,9},{9,10},{10,11},{11... | collective-permute-start | bytes 196616 | tf_op jit(solution)/shard_map/ppermute | solution.py:16
  103.3 15.6 %collective-permute-start.7 = (f32[1,128,128]{2,1,0:T(8,128)S(1)}, f32[1,128,128]{2,1,0:T(8,128)S(1)}, u32[]{:S(2)}, u32[]{:S(2)}) collective-permute-start(f32[1,128,128]{2,1,0:T(8,128)S(1)} %get-tuple-element.78), channel_id=1, source_target_pairs={{0,1},{1,2},{2,3},{3,4},{4,5},{5,6},{6,7},{8,9},{9,10},{10,11},{11... | collective-permute-start | bytes 196616 | tf_op jit(solution)/shard_map/ppermute | solution.py:16
  106.8 12.2 %collective-permute-start.6 = (f32[1,128,128]{2,1,0:T(8,128)S(1)}, f32[1,128,128]{2,1,0:T(8,128)S(1)}, u32[]{:S(2)}, u32[]{:S(2)}) collective-permute-start(f32[1,128,128]{2,1,0:T(8,128)S(1)} %get-tuple-element.79), channel_id=1, source_target_pairs={{1,0},{2,1},{3,2},{4,3},{5,4},{6,5},{7,6},{9,8},{10,9},{11,10},{12... | collective-permute-start | bytes 196616 | tf_op jit(solution)/shard_map/ppermute | solution.py:17
  126.7 17.0 %collective-permute-start.9 = (f32[1,128,128]{2,1,0:T(8,128)S(1)}, f32[1,128,128]{2,1,0:T(8,128)S(1)}, u32[]{:S(2)}, u32[]{:S(2)}) collective-permute-start(f32[1,128,128]{2,1,0:T(8,128)S(1)} %get-tuple-element.76), channel_id=1, source_target_pairs={{0,1},{1,2},{2,3},{3,4},{4,5},{5,6},{6,7},{8,9},{9,10},{10,11},{11... | collective-permute-start | bytes 196616 | tf_op jit(solution)/shard_map/ppermute | solution.py:16
  131.3 12.5 %collective-permute-start.8 = (f32[1,128,128]{2,1,0:T(8,128)S(1)}, f32[1,128,128]{2,1,0:T(8,128)S(1)}, u32[]{:S(2)}, u32[]{:S(2)}) collective-permute-start(f32[1,128,128]{2,1,0:T(8,128)S(1)} %get-tuple-element.77), channel_id=1, source_target_pairs={{1,0},{2,1},{3,2},{4,3},{5,4},{6,5},{7,6},{9,8},{10,9},{11,10},{12... | collective-permute-start | bytes 196616 | tf_op jit(solution)/shard_map/ppermute | solution.py:17
  151.5 16.9 %collective-permute-start.11 = (f32[1,128,128]{2,1,0:T(8,128)S(1)}, f32[1,128,128]{2,1,0:T(8,128)S(1)}, u32[]{:S(2)}, u32[]{:S(2)}) collective-permute-start(f32[1,128,128]{2,1,0:T(8,128)S(1)} %get-tuple-element.74), channel_id=1, source_target_pairs={{0,1},{1,2},{2,3},{3,4},{4,5},{5,6},{6,7},{8,9},{9,10},{10,11},{11... | collective-permute-start | bytes 196616 | tf_op jit(solution)/shard_map/ppermute | solution.py:16
  156.1 12.4 %collective-permute-start.10 = (f32[1,128,128]{2,1,0:T(8,128)S(1)}, f32[1,128,128]{2,1,0:T(8,128)S(1)}, u32[]{:S(2)}, u32[]{:S(2)}) collective-permute-start(f32[1,128,128]{2,1,0:T(8,128)S(1)} %get-tuple-element.75), channel_id=1, source_target_pairs={{1,0},{2,1},{3,2},{4,3},{5,4},{6,5},{7,6},{9,8},{10,9},{11,10},{12... | collective-permute-start | bytes 196616 | tf_op jit(solution)/shard_map/ppermute | solution.py:17
  179.7 15.3 %copy-start.40 = (f32[512]{0:T(512)S(1)}, f32[512]{0:T(512)}, u32[]{:S(2)}) copy-start(f32[512]{0:T(512)} %gather_fusion.1) | copy-start | bytes 6148
  188.6 6.9 %collective-permute-start.3 = (f32[1,128,128]{2,1,0:T(8,128)S(1)}, f32[1,128,128]{2,1,0:T(8,128)S(1)}, u32[]{:S(2)}, u32[]{:S(2)}) collective-permute-start(f32[1,128,128]{2,1,0:T(8,128)S(1)} %get-tuple-element.80), channel_id=1, source_target_pairs={{0,1},{1,2},{2,3},{3,4},{4,5},{5,6},{6,7},{8,9},{9,10},{10,11},{11... | collective-permute-start | bytes 196616 | tf_op jit(solution)/shard_map/ppermute | solution.py:16
  193.6 7.0 %collective-permute-start.2 = (f32[1,128,128]{2,1,0:T(8,128)S(1)}, f32[1,128,128]{2,1,0:T(8,128)S(1)}, u32[]{:S(2)}, u32[]{:S(2)}) collective-permute-start(f32[1,128,128]{2,1,0:T(8,128)S(1)} %get-tuple-element.81), channel_id=1, source_target_pairs={{1,0},{2,1},{3,2},{4,3},{5,4},{6,5},{7,6},{9,8},{10,9},{11,10},{12... | collective-permute-start | bytes 196616 | tf_op jit(solution)/shard_map/ppermute | solution.py:17
  213.7 6.7 %collective-permute-start.13 = (f32[1,128,128]{2,1,0:T(8,128)S(1)}, f32[1,128,128]{2,1,0:T(8,128)S(1)}, u32[]{:S(2)}, u32[]{:S(2)}) collective-permute-start(f32[1,128,128]{2,1,0:T(8,128)S(1)} %get-tuple-element.72), channel_id=1, source_target_pairs={{0,1},{1,2},{2,3},{3,4},{4,5},{5,6},{6,7},{8,9},{9,10},{10,11},{11... | collective-permute-start | bytes 196616 | tf_op jit(solution)/shard_map/ppermute | solution.py:16
  218.5 6.2 %collective-permute-start.12 = (f32[1,128,128]{2,1,0:T(8,128)S(1)}, f32[1,128,128]{2,1,0:T(8,128)S(1)}, u32[]{:S(2)}, u32[]{:S(2)}) collective-permute-start(f32[1,128,128]{2,1,0:T(8,128)S(1)} %get-tuple-element.73), channel_id=1, source_target_pairs={{1,0},{2,1},{3,2},{4,3},{5,4},{6,5},{7,6},{9,8},{10,9},{11,10},{12... | collective-permute-start | bytes 196616 | tf_op jit(solution)/shard_map/ppermute | solution.py:17
  234.5 4.7 %collective-permute-start.15 = (f32[1,128,128]{2,1,0:T(8,128)S(1)}, f32[1,128,128]{2,1,0:T(8,128)S(1)}, u32[]{:S(2)}, u32[]{:S(2)}) collective-permute-start(f32[1,128,128]{2,1,0:T(8,128)S(1)} %get-tuple-element.70), channel_id=1, source_target_pairs={{0,1},{1,2},{2,3},{3,4},{4,5},{5,6},{6,7},{8,9},{9,10},{10,11},{11... | collective-permute-start | bytes 196616 | tf_op jit(solution)/shard_map/ppermute | solution.py:16
  237.3 6.2 %collective-permute-start.14 = (f32[1,128,128]{2,1,0:T(8,128)S(1)}, f32[1,128,128]{2,1,0:T(8,128)S(1)}, u32[]{:S(2)}, u32[]{:S(2)}) collective-permute-start(f32[1,128,128]{2,1,0:T(8,128)S(1)} %get-tuple-element.71), channel_id=1, source_target_pairs={{1,0},{2,1},{3,2},{4,3},{5,4},{6,5},{7,6},{9,8},{10,9},{11,10},{12... | collective-permute-start | bytes 196616 | tf_op jit(solution)/shard_map/ppermute | solution.py:17
  253.4 5.7 %collective-permute-start.17 = (f32[1,128,128]{2,1,0:T(8,128)S(1)}, f32[1,128,128]{2,1,0:T(8,128)S(1)}, u32[]{:S(2)}, u32[]{:S(2)}) collective-permute-start(f32[1,128,128]{2,1,0:T(8,128)S(1)} %get-tuple-element.68), channel_id=1, source_target_pairs={{0,1},{1,2},{2,3},{3,4},{4,5},{5,6},{6,7},{8,9},{9,10},{10,11},{11... | collective-permute-start | bytes 196616 | tf_op jit(solution)/shard_map/ppermute | solution.py:16
  257.2 6.2 %collective-permute-start.16 = (f32[1,128,128]{2,1,0:T(8,128)S(1)}, f32[1,128,128]{2,1,0:T(8,128)S(1)}, u32[]{:S(2)}, u32[]{:S(2)}) collective-permute-start(f32[1,128,128]{2,1,0:T(8,128)S(1)} %get-tuple-element.69), channel_id=1, source_target_pairs={{1,0},{2,1},{3,2},{4,3},{5,4},{6,5},{7,6},{9,8},{10,9},{11,10},{12... | collective-permute-start | bytes 196616 | tf_op jit(solution)/shard_map/ppermute | solution.py:17
  292.0 76.4 %copy-start.1 = (s32[16,2]{0,1:T(2,128)S(1)}, s32[16,2]{0,1:T(2,128)}, u32[]{:S(2)}) copy-start(s32[16,2]{0,1:T(2,128)} %param.19) | copy-start | bytes 388
  (40 other events, 254.2 us)
Sparse Core Ops, SparseCore 0:
  11.1 75.2 all-gather.1
  290.9 77.3 reduce-scatter.1
where the time goes:
time: 378 us; the launch traced here: 375 us
  waiting for transfers between devices  149 us (39%)
  other arithmetic  93.6 us (25%)
  local copies, waits for them, and re-layouts  59.6 us (16%)
  starting transfers between devices  49.6 us (13%)
  between operations  23.8 us (6%)
    reduce_scatter x1, waiting for transfers between devices, shards(): lax.psum_scatter(embedded, 'shot', scatter_dimension=1, tiled=True)  72.4 us
    all_gather x1, waiting for transfers between devices, shards(): gathered = lax.all_gather(stacked, 'shot', axis=2, tiled=True)  56.8 us
    ppermute x9, starting transfers between devices, with_halo(): before = lax.ppermute(last, axis, up)  37.4 us
    gather x4, local copies, waits for them, and re-layouts, shards(): sampled = following.reshape(-1)[receiver_flat]  30.2 us
    scatter-add x8, other arithmetic, add_cells(): return field.reshape(-1).at[positions].add(amounts).reshape(shape)  25.3 us
    add x4, other arithmetic, shards(): following = 2.0 * current - before + kappa_window * spread  18.2 us
    ppermute x9, waiting for transfers between devices, with_halo(): after = lax.ppermute(first, axis, down)  17.9 us
    dynamic_update_slice x1, local copies, waits for them, and re-layouts, shards(): lax.dynamic_update_slice(jnp.zeros((depth_cells, own_rows * groups, model...  13.7 us
  transfers between devices with their start and end apart: 20, of which 10 were waited for; matrix products, arithmetic and copies ran while one was open for 13% of the time, Pallas kernels for 0%

commit v1 on v0

v1 whole, which is shorter than its diff:
```python
import functools

import jax
import jax.numpy as jnp
from jax import lax
from jax.experimental import pallas as pl
from jax.experimental.pallas import tpu as pltpu
from jax.sharding import PartitionSpec as P

MESH = pl.DeviceIdType.MESH
NT = 4
PAD = 8
CHUNK = 32
OFFSETS = ((2, 0), (2, 1), (1, 0), (3, 0), (1, 1), (3, 1), (0, 1))


def kernel(
    anchors,
    wavelet,
    source,
    kappa,
    buoyancy,
    wave,
    adjoint,
    cells,
    observed,
    grad_out,
    wave_out,
    adjoint_out,
    raw,
    pack,
    win,
    pb,
    pm,
    qb,
    kp,
    bz,
    fd,
    cr,
    cc,
    dg,
    wb,
    ab,
    kc,
    ob,
    sf,
    vb,
    gb,
    gc,
    gr,
    acc,
    pr,
    tmp,
    load_sem,
    swap_send,
    swap_recv,
    win_send,
    win_recv,
    halo_send,
    halo_recv,
    grad_send,
    grad_recv,
    out_sem,
):
    depth, own, side = kappa.shape
    ap = side // 2
    f32 = jnp.float32
    shot = lax.axis_index("shot")
    slab = lax.axis_index("slab")
    slabs = lax.axis_size("slab")
    half = shot // 8
    lane_group = shot % 8
    px = lane_group // 2
    pc = lane_group % 2
    partner = (shot + 8) % 16
    below = (slab + 1) % slabs
    above = (slab + slabs - 1) % slabs

    def peer(o):
        dx, dc = OFFSETS[o]
        return ((px + dx) % 4) * 2 + (pc + dc) % 2

    def origin(o):
        dx, dc = OFFSETS[o]
        return ((px + 4 - dx) % 4) * 2 + (pc + dc) % 2

    inner = pl.ds(PAD, ap)
    body = pl.ds(1, depth)
    loads = [
        pltpu.make_async_copy(buoyancy, raw.at[half, 0], load_sem.at[0]),
        pltpu.make_async_copy(kappa, raw.at[half, 1], load_sem.at[1]),
        pltpu.make_async_copy(wave.at[0, 1], pb.at[0, body, inner, :], load_sem.at[2]),
        pltpu.make_async_copy(wave.at[0, 0], pm, load_sem.at[3]),
        pltpu.make_async_copy(adjoint.at[0, 1], ab.at[1], load_sem.at[4]),
        pltpu.make_async_copy(adjoint.at[0, 0], ab.at[0], load_sem.at[5]),
    ]
    for copy in loads:
        copy.start()

    barrier = pltpu.get_barrier_semaphore()
    pl.semaphore_signal(barrier, inc=1, device_id={"shot": partner, "slab": slab}, device_id_type=MESH)
    pl.semaphore_signal(barrier, inc=1, device_id={"shot": shot, "slab": below}, device_id_type=MESH)
    pl.semaphore_signal(barrier, inc=1, device_id={"shot": shot, "slab": above}, device_id_type=MESH)
    for o in range(7):
        pl.semaphore_signal(
            barrier, inc=1, device_id={"shot": half * 8 + peer(o), "slab": slab}, device_id_type=MESH
        )
    pl.semaphore_wait(barrier, 10)

    swaps = []
    for i, ref in enumerate((buoyancy, kappa)):
        swaps.append(
            pltpu.make_async_remote_copy(
                src_ref=ref,
                dst_ref=raw.at[half, i],
                send_sem=swap_send.at[i],
                recv_sem=swap_recv.at[i],
                device_id={"shot": partner, "slab": slab},
                device_id_type=MESH,
            )
        )
        swaps[-1].start()

    def halo_pair(slot, first, last, low, high):
        up = pltpu.make_async_remote_copy(
            src_ref=first,
            dst_ref=high,
            send_sem=halo_send.at[slot, 0],
            recv_sem=halo_recv.at[slot, 0],
            device_id={"shot": shot, "slab": above},
            device_id_type=MESH,
        )
        down = pltpu.make_async_remote_copy(
            src_ref=last,
            dst_ref=low,
            send_sem=halo_send.at[slot, 1],
            recv_sem=halo_recv.at[slot, 1],
            device_id={"shot": shot, "slab": below},
            device_id_type=MESH,
        )
        return (up, down)

    def field_halo(slot, field, src=None):
        first = field.at[1, inner, :] if src is None else src.at[0]
        last = field.at[depth, inner, :] if src is None else src.at[depth - 1]
        return halo_pair(
            slot, first, last, field.at[0, inner, :], field.at[depth + 1, inner, :]
        )

    halos = [field_halo(0, pb.at[0], wave.at[0, 1])]
    halos += [field_halo(n, pb.at[n]) for n in range(1, NT)]
    halos += [field_halo(NT + m, wb.at[m]) for m in range(NT)]
    halos.append(field_halo(2 * NT, bz))

    def go(pair):
        pair[0].start()
        pair[1].start()

    def arrived(pair):
        pair[0].wait_recv()
        pair[1].wait_recv()

    go(halos[0])

    margin = jnp.zeros((PAD, ap), f32)

    def clear(i, carry):
        for n in range(NT):
            pb[n, i + 1, :PAD, :] = margin
            pb[n, i + 1, PAD + ap :, :] = margin
            wb[n, i + 1, :PAD, :] = margin
            wb[n, i + 1, PAD + ap :, :] = margin
        bz[i + 1, :PAD, :] = margin
        bz[i + 1, PAD + ap :, :] = margin
        cr[i, PAD + ap :, :] = margin
        return carry

    lax.fori_loop(0, depth, clear, 0)

    count = cells.shape[1]
    rows_at = lax.broadcasted_iota(jnp.int32, (ap, ap), 0)
    lanes_at = lax.broadcasted_iota(jnp.int32, (ap, ap), 1)
    flat = (cells[0:1, :] - slab * depth) * ap + cells[1:2, :]
    column = cells[2:3, :]
    hit = column == lax.broadcasted_iota(jnp.int32, (ap, count), 0)

    def place(row, values):
        vb[row : row + ap, :] = jnp.where(hit, values, 0.0).astype(jnp.bfloat16)

    for n in range(NT):
        rest = observed[n : n + 1, :]
        base = (n // 2) * 6 * ap + (n % 2) * ap
        for part in range(3):
            top = rest.astype(jnp.bfloat16).astype(f32)
            place(base + part * 2 * ap, top)
            rest = rest - top
    place(12 * ap, jnp.ones((1, count), f32))
    group = 4

    def spot(ch, carry):
        at = lax.broadcasted_iota(jnp.int32, (group * ap, count), 0) + ch * (group * ap)
        onehot = jnp.where(flat == at, 1.0, 0.0).astype(jnp.bfloat16)

        def times(row, width):
            return lax.dot_general(
                onehot, vb[row : row + width, :], (((1,), (1,)), ((), ())), preferred_element_type=f32
            )

        for pair in range(NT // 2):
            total = times(pair * 6 * ap, 2 * ap)
            total = total + times(pair * 6 * ap + 2 * ap, 2 * ap)
            total = total + times(pair * 6 * ap + 4 * ap, 2 * ap)
            total = total.reshape(group, ap, 2 * ap)
            ob[2 * pair, pl.ds(ch * group, group), :, :] = total[:, :, :ap]
            ob[2 * pair + 1, pl.ds(ch * group, group), :, :] = total[:, :, ap:]
        kc[pl.ds(ch * group, group), :, :] = times(12 * ap, ap).reshape(group, ap, ap)
        return carry

    lax.fori_loop(0, depth // group, spot, 0)

    def mark(d, carry):
        here = (rows_at == source[0, 1]) & (lanes_at == source[0, 2])
        deep = jnp.where(source[0, 0] == slab * depth + d, 1.0, 0.0)
        sf[d, :, :] = jnp.where(here, deep, 0.0)
        return carry

    lax.fori_loop(0, depth, mark, 0)

    my_rows = lax.broadcasted_iota(jnp.int32, (own, ap), 0) + lane_group * own
    my_lanes = lax.broadcasted_iota(jnp.int32, (own, ap), 1)
    home = pl.ds(pl.multiple_of(lane_group * own, own), own)

    def window_copy(i, o, spot_rows):
        return pltpu.make_async_remote_copy(
            src_ref=pack.at[i, o],
            dst_ref=win.at[i, :, spot_rows, :],
            send_sem=win_send.at[i, o],
            recv_sem=win_recv.at[i, o],
            device_id={"shot": half * 8 + peer(o), "slab": slab},
            device_id_type=MESH,
        )

    def rows_of(member):
        return pl.ds(pl.multiple_of(member * own, own), own)

    for i in range(2):
        loads[i].wait()
        swaps[i].wait_recv()

        def fill(d, carry):
            low = raw[0, i, d]
            high = raw[1, i, d]
            for o in range(8):
                member = half * 8 + (peer(o) if o < 7 else lane_group)
                keep_row = my_rows >= anchors[member, 0]
                keep_col = my_lanes >= anchors[member, 1]
                a = jnp.where(keep_col, low[:, :ap], low[:, ap:])
                b = jnp.where(keep_col, high[:, :ap], high[:, ap:])
                value = jnp.where(keep_row, a, b)
                if o < 7:
                    pack[i, o, d] = value
                else:
                    win[i, d, home, :] = value
            return carry

        lax.fori_loop(0, depth, fill, 0)
        for o in range(7):
            window_copy(i, o, home).start()

    row_anchor = anchors[shot, 0]
    col_anchor = anchors[shot, 1]

    def unwind(x, lane_shift, first_row):
        x = pltpu.roll(x, lane_shift, axis=1)
        tmp[:ap, :] = x
        tmp[ap:, :] = x
        return tmp[pl.ds(first_row, ap), :]

    back = (ap - col_anchor) % ap

    for o in range(7):
        window_copy(0, o, rows_of(origin(o))).wait_recv()

    def settle_buoyancy(d, carry):
        bz[d + 1, inner, :] = unwind(win[0, d], back, row_anchor)
        return carry

    lax.fori_loop(0, depth, settle_buoyancy, 0)
    go(halos[2 * NT])

    def sides(d, carry):
        for c0 in range(0, ap, CHUNK):
            rows = lax.broadcasted_iota(jnp.int32, (CHUNK, ap), 0) + c0
            lanes = lax.broadcasted_iota(jnp.int32, (CHUNK, ap), 1)
            x = bz[d + 1, PAD + c0 : PAD + c0 + CHUNK, :]
            prev = bz[d + 1, PAD + c0 - 1 : PAD + c0 - 1 + CHUNK, :]
            succ = bz[d + 1, PAD + c0 + 1 : PAD + c0 + 1 + CHUNK, :]
            face = 0.5 * (x + prev)
            total = face + 0.5 * (x + succ)
            cr[d, PAD + c0 : PAD + c0 + CHUNK, :] = jnp.where(rows == 0, 0.0, face)
            prev = jnp.where(lanes == 0, 0.0, pltpu.roll(x, 1, axis=1))
            succ = jnp.where(lanes == ap - 1, 0.0, pltpu.roll(x, ap - 1, axis=1))
            face = 0.5 * (x + prev)
            total = total + face + 0.5 * (x + succ)
            cc[d, c0 : c0 + CHUNK, :] = jnp.where(lanes == 0, 0.0, face)
            dg[d, c0 : c0 + CHUNK, :] = total
        return carry

    lax.fori_loop(0, depth, sides, 0)
    arrived(halos[2 * NT])

    def depths(d, carry):
        first = (slab == 0) & (d == 0)
        last = (slab == slabs - 1) & (d == depth - 1)
        for c0 in range(0, ap, CHUNK):
            span = slice(PAD + c0, PAD + c0 + CHUNK)
            x = bz[d + 1, span, :]
            prev = jnp.where(first, 0.0, bz[d, span, :])
            succ = jnp.where(last, 0.0, bz[d + 2, span, :])
            low = 0.5 * (x + prev)
            high = 0.5 * (x + succ)
            fd[d, c0 : c0 + CHUNK, :] = jnp.where(first, 0.0, low)
            fd[d + 1, c0 : c0 + CHUNK, :] = jnp.where(last, 0.0, high)
            dg[d, c0 : c0 + CHUNK, :] = dg[d, c0 : c0 + CHUNK, :] + low + high
        return carry

    lax.fori_loop(0, depth, depths, 0)

    def spread(field, d, c0):
        at = PAD + c0
        x = field[d + 1, at : at + CHUNK, :]
        across = cc[d, c0 : c0 + CHUNK, :]
        total = fd[d, c0 : c0 + CHUNK, :] * field[d, at : at + CHUNK, :]
        total = total + fd[d + 1, c0 : c0 + CHUNK, :] * field[d + 2, at : at + CHUNK, :]
        total = total + cr[d, at : at + CHUNK, :] * field[d + 1, at - 1 : at - 1 + CHUNK, :]
        total = total + cr[d, at + 1 : at + 1 + CHUNK, :] * field[d + 1, at + 1 : at + 1 + CHUNK, :]
        total = total + across * pltpu.roll(x, 1, axis=1)
        total = total + pltpu.roll(across * x, ap - 1, axis=1)
        return total - dg[d, c0 : c0 + CHUNK, :] * x, x

    def edges_first(step, after):
        lax.fori_loop(0, 2, lambda i, c: step(i * (depth - 1), c), 0)
        after()
        lax.fori_loop(1, depth - 1, step, 0)

    loads[2].wait()
    loads[3].wait()
    arrived(halos[0])

    def first_spread(d, carry):
        for c0 in range(0, ap, CHUNK):
            qb[0, d, c0 : c0 + CHUNK, :] = spread(pb.at[0], d, c0)[0]
        return carry

    lax.fori_loop(0, depth, first_spread, 0)

    for o in range(7):
        window_copy(1, o, rows_of(origin(o))).wait_recv()
    loads[4].wait()
    loads[5].wait()

    def first_step(d, carry):
        kp[d] = unwind(win[1, d], back, row_anchor)
        for c0 in range(0, ap, CHUNK):
            rows = slice(c0, c0 + CHUNK)
            at = slice(PAD + c0, PAD + c0 + CHUNK)
            k = kp[d, rows, :]
            nxt = 2.0 * pb[0, d + 1, at, :] - pm[d, rows, :] + k * qb[0, d, rows, :]
            pb[1, d + 1, at, :] = nxt + wavelet[0, 0] * sf[d, rows, :]
            wb[0, d + 1, at, :] = k * ab[1, d, rows, :]
        return carry

    def send_first():
        go(halos[1])
        go(halos[NT])

    edges_first(first_step, send_first)

    for n in range(1, NT):

        def forward(d, carry):
            for c0 in range(0, ap, CHUNK):
                rows = slice(c0, c0 + CHUNK)
                at = slice(PAD + c0, PAD + c0 + CHUNK)
                q, x = spread(pb.at[n], d, c0)
                qb[n, d, rows, :] = q
                nxt = 2.0 * x - pb[n - 1, d + 1, at, :] + kp[d, rows, :] * q
                pb[n + 1, d + 1, at, :] = nxt + wavelet[0, n] * sf[d, rows, :]
            return carry

        arrived(halos[n])
        edges_first(forward, (lambda: go(halos[n + 1])) if n + 1 < NT else (lambda: None))

    outs = [
        pltpu.make_async_copy(pb.at[NT - 1, body, inner, :], wave_out.at[0, 0], out_sem.at[0]),
        pltpu.make_async_copy(pb.at[NT, body, inner, :], wave_out.at[0, 1], out_sem.at[1]),
    ]
    outs[0].start()
    outs[1].start()

    for m in range(NT):
        n = NT - m

        def backward(d, carry):
            for c0 in range(0, ap, CHUNK):
                rows = slice(c0, c0 + CHUNK)
                at = slice(PAD + c0, PAD + c0 + CHUNK)
                q, _ = spread(wb.at[m], d, c0)
                now = 2.0 * ab[m + 1, d, rows, :] - ab[m, d, rows, :] + q
                now = now + (kc[d, rows, :] * pb[n, d + 1, at, :] - ob[n - 1, d, rows, :])
                ab[m + 2, d, rows, :] = now
                if n > 1:
                    wb[m + 1, d + 1, at, :] = kp[d, rows, :] * now
                term = now * qb[n - 1, d, rows, :]
                gb[d, rows, :] = term if m == 0 else gb[d, rows, :] + term
            return carry

        arrived(halos[NT + m])
        edges_first(backward, (lambda: go(halos[NT + m + 1])) if n > 1 else (lambda: None))

    outs += [
        pltpu.make_async_copy(ab.at[NT], adjoint_out.at[0, 0], out_sem.at[2]),
        pltpu.make_async_copy(ab.at[NT + 1], adjoint_out.at[0, 1], out_sem.at[3]),
    ]
    outs[2].start()
    outs[3].start()

    def wind(d, carry):
        gc[d] = unwind(gb[d], col_anchor % ap, ap - row_anchor)
        return carry

    lax.fori_loop(0, depth, wind, 0)

    def grad_copy(o, spot_rows):
        return pltpu.make_async_remote_copy(
            src_ref=gc.at[:, spot_rows, :],
            dst_ref=gr.at[o],
            send_sem=grad_send.at[o],
            recv_sem=grad_recv.at[o],
            device_id={"shot": half * 8 + peer(o), "slab": slab},
            device_id_type=MESH,
        )

    for o in range(7):
        grad_copy(o, rows_of(peer(o))).start()
    for o in range(7):
        grad_copy(o, rows_of(peer(o))).wait_recv()

    def collect(d, carry):
        parts = [jnp.zeros((own, ap), f32) for _ in range(4)]
        for o in range(8):
            value = gr[o, d] if o < 7 else gc[d, home, :]
            member = half * 8 + (origin(o) if o < 7 else lane_group)
            keep_row = my_rows >= anchors[member, 0]
            keep_col = my_lanes >= anchors[member, 1]
            low = jnp.where(keep_row, value, 0.0)
            high = jnp.where(keep_row, 0.0, value)
            parts[0] += jnp.where(keep_col, low, 0.0)
            parts[1] += jnp.where(keep_col, 0.0, low)
            parts[2] += jnp.where(keep_col, high, 0.0)
            parts[3] += jnp.where(keep_col, 0.0, high)
        acc[0, d, :, :ap] = parts[0]
        acc[0, d, :, ap:] = parts[1]
        acc[1, d, :, :ap] = parts[2]
        acc[1, d, :, ap:] = parts[3]
        return carry

    lax.fori_loop(0, depth, collect, 0)
    merge = pltpu.make_async_remote_copy(
        src_ref=acc.at[1 - half],
        dst_ref=pr,
        send_sem=swap_send.at[2],
        recv_sem=swap_recv.at[2],
        device_id={"shot": partner, "slab": slab},
        device_id_type=MESH,
    )
    merge.start()
    merge.wait_recv()

    def finish(d, carry):
        pr[d] = pr[d] + acc[half, d]
        return carry

    lax.fori_loop(0, depth, finish, 0)
    outs.append(pltpu.make_async_copy(pr, grad_out, out_sem.at[4]))
    outs[4].start()

    for swap in swaps:
        swap.wait_send()
    merge.wait_send()
    for pair in halos:
        pair[0].wait_send()
        pair[1].wait_send()
    for o in range(7):
        window_copy(0, o, home).wait_send()
        window_copy(1, o, home).wait_send()
        grad_copy(o, rows_of(peer(o))).wait_send()
    for copy in outs:
        copy.wait()


def shards(
    kappa,
    buoyancy,
    anchors,
    wave_start,
    adjoint_start,
    wavelet,
    source_cell,
    receiver_cells,
    observed,
):
    depth, own, side = kappa.shape
    ap = wave_start.shape[3]
    count = receiver_cells.shape[1]
    f32 = jnp.float32
    any_space = pl.BlockSpec(memory_space=pl.ANY)
    smem = pl.BlockSpec(memory_space=pltpu.SMEM)
    vmem = pl.BlockSpec(memory_space=pltpu.VMEM)
    padded = (depth + 2, ap + 2 * PAD, ap)
    plain = (depth, ap, ap)
    return pl.pallas_call(
        kernel,
        out_shape=(
            jax.ShapeDtypeStruct(kappa.shape, f32),
            jax.ShapeDtypeStruct(wave_start.shape, f32),
            jax.ShapeDtypeStruct(adjoint_start.shape, f32),
        ),
        in_specs=[smem, smem, smem, any_space, any_space, any_space, any_space, vmem, vmem],
        out_specs=(any_space, any_space, any_space),
        scratch_shapes=[
            pltpu.VMEM((2, 2, depth, own, side), f32),
            pltpu.VMEM((2, 7, depth, own, ap), f32),
            pltpu.VMEM((2,) + plain, f32),
            pltpu.VMEM((NT + 1,) + padded, f32),
            pltpu.VMEM(plain, f32),
            pltpu.VMEM((NT,) + plain, f32),
            pltpu.VMEM(plain, f32),
            pltpu.VMEM(padded, f32),
            pltpu.VMEM((depth + 1, ap, ap), f32),
            pltpu.VMEM((depth, ap + 2 * PAD, ap), f32),
            pltpu.VMEM(plain, f32),
            pltpu.VMEM(plain, f32),
            pltpu.VMEM((NT,) + padded, f32),
            pltpu.VMEM((NT + 2,) + plain, f32),
            pltpu.VMEM(plain, f32),
            pltpu.VMEM((NT,) + plain, f32),
            pltpu.VMEM(plain, f32),
            pltpu.VMEM((13 * ap, count), jnp.bfloat16),
            pltpu.VMEM(plain, f32),
            pltpu.VMEM(plain, f32),
            pltpu.VMEM((7, depth, own, ap), f32),
            pltpu.VMEM((2, depth, own, side), f32),
            pltpu.VMEM((depth, own, side), f32),
            pltpu.VMEM((2 * ap, ap), f32),
            pltpu.SemaphoreType.DMA((6,)),
            pltpu.SemaphoreType.DMA((3,)),
            pltpu.SemaphoreType.DMA((3,)),
            pltpu.SemaphoreType.DMA((2, 7)),
            pltpu.SemaphoreType.DMA((2, 7)),
            pltpu.SemaphoreType.DMA((2 * NT + 1, 2)),
            pltpu.SemaphoreType.DMA((2 * NT + 1, 2)),
            pltpu.SemaphoreType.DMA((7,)),
            pltpu.SemaphoreType.DMA((7,)),
            pltpu.SemaphoreType.DMA((5,)),
        ],
        compiler_params=pltpu.CompilerParams(
            collective_id=0, has_side_effects=True, vmem_limit_bytes=60 * 1024 * 1024
        ),
    )(
        anchors,
        wavelet,
        source_cell,
        kappa,
        buoyancy,
        wave_start,
        adjoint_start,
        receiver_cells[0].T,
        observed[0],
    )


def solution(mesh):
    in_specs = (
        P("slab", "shot", None),
        P("slab", "shot", None),
        P(),
        P("shot", None, "slab", None, None),
        P("shot", None, "slab", None, None),
        P("shot", None),
        P("shot", None),
        P("shot", None, None),
        P("shot", None, None),
    )
    out_specs = (
        P("slab", "shot", None),
        P("shot", None, "slab", None, None),
        P("shot", None, "slab", None, None),
    )
    return jax.shard_map(shards, mesh=mesh, in_specs=in_specs, out_specs=out_specs, check_vma=False)
```

time: 378 us -> 108 us (0.29)
  waiting for transfers between devices: 149 us -> 0 us
  Pallas kernels: 0 us -> 96.7 us
  other arithmetic: 93.6 us -> 0 us
  local copies, waits for them, and re-layouts: 59.6 us -> 8.92 us
  starting transfers between devices: 49.6 us -> 0 us
  between operations: 23.8 us -> 0.64 us
    pallas_call x0 -> x1, Pallas kernels: none -> 96.7 us  [shards(): pl.pallas_call(kernel, out_shape=(jax.ShapeDtypeStruct(kappa.shape, f32),...]
    reduce_scatter x1 -> x0, waiting for transfers between devices: 72.4 us -> none  [shards(): lax.psum_scatter(embedded, 'shot', scatter_dimension=1, tiled=True)]
    all_gather x1 -> x0, waiting for transfers between devices: 56.8 us -> none  [shards(): gathered = lax.all_gather(stacked, 'shot', axis=2, tiled=True)]
    ppermute x18 -> x0, starting transfers between devices: 49.5 us -> none  [the longest x9 37.4 us: with_halo(): before = lax.ppermute(last, axis, up)]
    mul x27 -> x0, other arithmetic: 31.7 us -> none  [the longest x8 11 us: spread_of(): flux = col_face * (pad_cols[:, :, 1:] - pad_cols[:, :, :-1])]
    gather x4 -> x0, local copies, waits for them, and re-layouts: 30.2 us -> none  [shards(): sampled = following.reshape(-1)[receiver_flat]]
    add x9 -> x0, other arithmetic: 30.2 us -> none  [the longest x4 18.2 us: shards(): following = 2.0 * current - before + kappa_window * spread]
    scatter-add x8 -> x0, other arithmetic: 25.3 us -> none  [add_cells(): return field.reshape(-1).at[positions].add(amounts).reshape(shape)]
  transfers between devices with their start and end apart: 20 -> 0, of which waited for: 10 -> 0; matrix products, arithmetic and copies ran while one was open for 13% -> 0% of each run, Pallas kernels for 0% -> 0%
where the time goes in v1:
time: 108 us; the launch traced here: 106 us
  Pallas kernels  96.7 us (90%)
  local copies, waits for them, and re-layouts  8.92 us (8%)
    pallas_call x1, Pallas kernels, shards(): pl.pallas_call(kernel, out_shape=(jax.ShapeDtypeStruct(kappa.shape, f32),...  96.7 us
    unnamed x7, local copies, waits for them, and re-layouts  8.92 us

profile of v1, /device:TPU:0, one launch (start us, length us, event | category | flops | bytes accessed | tf_op | source)
XLA Modules:
  0.0 106.3 jit_solution(13880104384116556061)
XLA Ops:
  0.6 1.4 %copy.12.anchors = s32[16,2]{1,0:T(8,128)} copy(s32[16,2]{0,1:T(2,128)} %param.11) | data formatting | bytes 256 | tf_op args[2]
  2.0 1.3 %copy.15 = s32[1,512,3]{1,2,0:T(4,128)} copy(s32[1,512,3]{1,0,2:T(1,128)} %param.16) | data formatting | bytes 12288
  3.3 96.7 %shard_map.112 = (f32[16,16,256]{2,1,0:T(8,128)}, f32[1,2,16,128,128]{4,3,2,1,0:T(8,128)}, f32[1,2,16,128,128]{4,3,2,1,0:T(8,128)}) custom-call(s32[16,2]{1,0:T(8,128)} %copy.12.anchors, f32[1,4]{1,0:T(1,128)} %wavelet.1, s32[1,3]{1,0:T(1,128)} %source.1, f32[16,16,256]{2,1,0:T(8,128)} %kappa.1, f32[16,16,256]{2,1,0:T(8,128)} %buoyancy.1, ...), custom_call_target="tpu_custom_call" | custom-call | tf_op jit(solution)/shard_map/pallas_call | solution.py:522
  100.0 1.7 %copy.19 = f32[16,16,256]{2,1,0:T(8,128)} copy(f32[16,16,256]{2,1,0:T(8,128)} %get-tuple-element.6) | data formatting | bytes 524288
  101.7 0.0 copy-start
  101.7 3.3 %copy.20 = f32[1,2,16,128,128]{4,3,2,1,0:T(8,128)} copy(f32[1,2,16,128,128]{4,3,2,1,0:T(8,128)} %get-tuple-element.7) | data formatting | bytes 4194304
  105.0 0.0 copy-done
  105.0 1.3 %copy.21 = f32[1,2,16,128,128]{4,3,2,1,0:T(8,128)} copy(f32[1,2,16,128,128]{4,3,2,1,0:T(8,128)S(1)} %copy-done) | data formatting | bytes 4194304
Async XLA Ops:
  101.7 3.3 %copy-start = (f32[1,2,16,128,128]{4,3,2,1,0:T(8,128)S(1)}, f32[1,2,16,128,128]{4,3,2,1,0:T(8,128)}, u32[]{:S(2)}) copy-start(f32[1,2,16,128,128]{4,3,2,1,0:T(8,128)} %get-tuple-element.8) | copy-start | bytes 6291460

commit v2 on v1

v2 whole, which is shorter than its diff:
```python
import jax
import jax.numpy as jnp
from jax import lax
from jax.experimental import pallas as pl
from jax.experimental.pallas import tpu as pltpu
from jax.sharding import PartitionSpec as P

MESH = pl.DeviceIdType.MESH
NT = 4
PAD = 8
CHUNK = 32
OFFSETS = ((2, 0), (2, 1), (1, 0), (3, 0), (1, 1), (3, 1), (0, 1))


def kernel(
    anchors,
    wavelet,
    source,
    kappa,
    buoyancy,
    wave,
    adjoint,
    cells,
    observed,
    grad_out,
    wave_out,
    adjoint_out,
    raw,
    pack,
    win,
    pb,
    qb,
    kp,
    bz,
    fd,
    cr,
    cc,
    dg,
    wb,
    ab,
    kc,
    ob,
    sf,
    vb,
    gb,
    gc,
    gr,
    acc,
    pr,
    tmp,
    load_sem,
    swap_send,
    swap_recv,
    win_send,
    win_recv,
    halo_send,
    halo_recv,
    grad_send,
    grad_recv,
    merge_send,
    merge_recv,
    out_sem,
):
    depth, own, side = kappa.shape
    ap = side // 2
    f32 = jnp.float32
    shot = lax.axis_index("shot")
    slab = lax.axis_index("slab")
    slabs = lax.axis_size("slab")
    half = shot // 8
    lane_group = shot % 8
    px = lane_group // 2
    pc = lane_group % 2
    partner = (shot + 8) % 16
    below = (slab + 1) % slabs
    above = (slab + slabs - 1) % slabs
    parts = depth // 4

    def peer(o):
        dx, dc = OFFSETS[o]
        return ((px + dx) % 4) * 2 + (pc + dc) % 2

    def origin(o):
        dx, dc = OFFSETS[o]
        return ((px + 4 - dx) % 4) * 2 + (pc + 2 - dc) % 2

    sent = []
    due = []

    def start_local(copy):
        copy.start()
        due.append((copy, copy.wait))

    def start_remote(copy):
        copy.start()
        sent.append(copy.wait_send)
        due.append((copy, copy.wait_recv))

    def finish_of(copy):
        for i, (known, wait) in enumerate(due):
            if known is copy or (isinstance(copy, tuple) and known == copy):
                due.pop(i)
                wait()
                return
        raise ValueError(copy)

    def remote(src, dst, send, recv, to_shot, to_slab):
        return pltpu.make_async_remote_copy(
            src_ref=src,
            dst_ref=dst,
            send_sem=send,
            recv_sem=recv,
            device_id={"shot": to_shot, "slab": to_slab},
            device_id_type=MESH,
        )

    inner = pl.ds(PAD, ap)
    body = pl.ds(1, depth)

    barrier = pltpu.get_barrier_semaphore()

    def greet(to_shot, to_slab):
        pl.semaphore_signal(
            barrier, inc=1, device_id={"shot": to_shot, "slab": to_slab}, device_id_type=MESH
        )

    greet(partner, slab)
    greet(shot, below)
    greet(shot, above)
    for o in range(7):
        greet(half * 8 + peer(o), slab)

    loads = [
        pltpu.make_async_copy(buoyancy, raw.at[half, 0], load_sem.at[0]),
        pltpu.make_async_copy(kappa, raw.at[half, 1], load_sem.at[1]),
        pltpu.make_async_copy(wave.at[0, 0], pb.at[0, body, inner, :], load_sem.at[2]),
        pltpu.make_async_copy(wave.at[0, 1], pb.at[1, body, inner, :], load_sem.at[3]),
        pltpu.make_async_copy(adjoint.at[0, 0], ab.at[0], load_sem.at[4]),
        pltpu.make_async_copy(adjoint.at[0, 1], ab.at[1], load_sem.at[5]),
    ]
    for copy in loads:
        start_local(copy)

    margin = jnp.zeros((PAD, ap), f32)

    def clear(i, carry):
        for n in range(NT):
            pb[n + 1, i + 1, :PAD, :] = margin
            pb[n + 1, i + 1, PAD + ap :, :] = margin
            wb[n, i + 1, :PAD, :] = margin
            wb[n, i + 1, PAD + ap :, :] = margin
        bz[i + 1, :PAD, :] = margin
        bz[i + 1, PAD + ap :, :] = margin
        cr[i, PAD + ap :, :] = margin
        return carry

    lax.fori_loop(0, depth, clear, 0)

    count = cells.shape[2]
    rows_at = lax.broadcasted_iota(jnp.int32, (ap, ap), 0)
    lanes_at = lax.broadcasted_iota(jnp.int32, (ap, ap), 1)
    flat = (cells[0] - slab * depth) * ap + cells[1]
    hit = cells[2] == lax.broadcasted_iota(jnp.int32, (ap, count), 0)

    def place(row, values):
        vb[row : row + ap, :] = jnp.where(hit, values, 0.0).astype(jnp.bfloat16)

    for n in range(NT):
        rest = observed[n : n + 1, :]
        base = (n // 2) * 6 * ap + (n % 2) * ap
        for part in range(3):
            top = rest.astype(jnp.bfloat16).astype(f32)
            place(base + part * 2 * ap, top)
            rest = rest - top
    place(12 * ap, jnp.ones((1, count), f32))

    def mark(d, carry):
        here = (rows_at == source[0, 1]) & (lanes_at == source[0, 2])
        deep = jnp.where(source[0, 0] == slab * depth + d, 1.0, 0.0)
        sf[d, :, :] = jnp.where(here, deep, 0.0)
        return carry

    lax.fori_loop(0, depth, mark, 0)

    group = depth // parts

    def spot(ch):
        at = lax.broadcasted_iota(jnp.int32, (group * ap, count), 0) + ch * (group * ap)
        onehot = jnp.where(flat == at, 1.0, 0.0).astype(jnp.bfloat16)

        def times(row, width):
            return lax.dot_general(
                onehot, vb[row : row + width, :], (((1,), (1,)), ((), ())), preferred_element_type=f32
            )

        for pair in range(NT // 2):
            total = times(pair * 6 * ap, 2 * ap)
            total = total + times(pair * 6 * ap + 2 * ap, 2 * ap)
            total = total + times(pair * 6 * ap + 4 * ap, 2 * ap)
            total = total.reshape(group, ap, 2 * ap)
            ob[2 * pair, pl.ds(ch * group, group), :, :] = total[:, :, :ap]
            ob[2 * pair + 1, pl.ds(ch * group, group), :, :] = total[:, :, ap:]
        kc[pl.ds(ch * group, group), :, :] = times(12 * ap, ap).reshape(group, ap, ap)

    pl.semaphore_wait(barrier, 10)

    def plane_of(q, p):
        return 2 * q + p + (p // 2) * (depth - 4 - 4 * q)

    swaps = []
    for q in range(parts):
        swaps.append([])
        for i, ref in enumerate((buoyancy, kappa)):
            for e in range(2):
                planes = pl.ds(plane_of(q, 2 * e), 2)
                swaps[q].append(
                    remote(
                        ref.at[planes],
                        raw.at[half, i, planes],
                        swap_send.at[q, i, e],
                        swap_recv.at[q, i, e],
                        partner,
                        slab,
                    )
                )

    def swap_part(q):
        for copy in swaps[q]:
            start_remote(copy)

    def field_halo(slot, field, src=None):
        first = field.at[1, inner, :] if src is None else src.at[0]
        last = field.at[depth, inner, :] if src is None else src.at[depth - 1]
        return (
            remote(
                first,
                field.at[depth + 1, inner, :],
                halo_send.at[slot, 0],
                halo_recv.at[slot, 0],
                shot,
                above,
            ),
            remote(
                last,
                field.at[0, inner, :],
                halo_send.at[slot, 1],
                halo_recv.at[slot, 1],
                shot,
                below,
            ),
        )

    wave_halo = [field_halo(0, pb.at[1], wave.at[0, 1])]
    wave_halo += [field_halo(n, pb.at[n + 1]) for n in range(1, NT)]
    back_halo = [field_halo(NT + m, wb.at[m]) for m in range(NT)]
    buoy_halo = field_halo(2 * NT, bz)

    def go(pair):
        start_remote(pair[0])
        start_remote(pair[1])

    def arrived(pair):
        finish_of(pair[0])
        finish_of(pair[1])

    swap_part(0)
    swap_part(1)

    my_rows = lax.broadcasted_iota(jnp.int32, (own, ap), 0) + lane_group * own
    my_lanes = lax.broadcasted_iota(jnp.int32, (own, ap), 1)

    def rows_of(member):
        return pl.ds(pl.multiple_of(member * own, own), own)

    home = rows_of(lane_group)

    def window_copy(q, o, spot_rows):
        return remote(
            pack.at[q, o],
            win.at[q, :, :, spot_rows, :],
            win_send.at[q, o],
            win_recv.at[q, o],
            half * 8 + peer(o),
            slab,
        )

    finish_of(loads[0])
    finish_of(loads[1])
    for q in range(parts):
        for copy in swaps[q]:
            finish_of(copy)

        def fill(p, carry):
            d = plane_of(q, p)
            for i in range(2):
                low = raw[0, i, d]
                high = raw[1, i, d]
                for o in range(8):
                    member = half * 8 + (peer(o) if o < 7 else lane_group)
                    keep_row = my_rows >= anchors[0, member]
                    keep_col = my_lanes >= anchors[1, member]
                    a = jnp.where(keep_col, low[:, :ap], low[:, ap:])
                    b = jnp.where(keep_col, high[:, :ap], high[:, ap:])
                    value = jnp.where(keep_row, a, b)
                    if o < 7:
                        pack[q, o, i, p] = value
                    else:
                        win[q, i, p, home, :] = value
            return carry

        lax.fori_loop(0, 4, fill, 0)
        for o in range(7):
            copy = window_copy(q, o, home)
            copy.start()
            sent.append(copy.wait_send)
            landing = window_copy(q, o, rows_of(origin(o)))
            due.append(((q, o), landing.wait_recv))
        if q + 2 < parts:
            swap_part(q + 2)
        elif q + 2 == parts:
            go(wave_halo[0])
        spot(q)

    row_anchor = anchors[0, shot]
    col_anchor = anchors[1, shot]

    def unwind(x, lane_shift, first_row):
        x = pltpu.roll(x, lane_shift, axis=1)
        tmp[:ap, :] = x
        tmp[ap:, :] = x
        return tmp[pl.ds(first_row, ap), :]

    lane_back = (ap - col_anchor) % ap

    def settle(q):
        for o in range(7):
            finish_of((q, o))

        def one(p, carry):
            d = plane_of(q, p)
            bz[d + 1, inner, :] = unwind(win[q, 0, p], lane_back, row_anchor)
            k = unwind(win[q, 1, p], lane_back, row_anchor)
            kp[d] = k
            wb[0, d + 1, inner, :] = k * ab[1, d]
            return carry

        lax.fori_loop(0, 4, one, 0)

    def each(low, high, step):
        def both(i, carry):
            d = low + i // 2
            step(d + (i % 2) * (depth - 1 - 2 * d))
            return carry

        lax.fori_loop(0, 2 * (high - low), both, 0)

    def coefficients(d):
        first = (slab == 0) & (d == 0)
        last = (slab == slabs - 1) & (d == depth - 1)
        for c0 in range(0, ap, CHUNK):
            rows = lax.broadcasted_iota(jnp.int32, (CHUNK, ap), 0) + c0
            lanes = lax.broadcasted_iota(jnp.int32, (CHUNK, ap), 1)
            at = slice(PAD + c0, PAD + c0 + CHUNK)
            x = bz[d + 1, at, :]
            prev = bz[d + 1, PAD + c0 - 1 : PAD + c0 - 1 + CHUNK, :]
            succ = bz[d + 1, PAD + c0 + 1 : PAD + c0 + 1 + CHUNK, :]
            face = 0.5 * (x + prev)
            total = face + 0.5 * (x + succ)
            cr[d, at, :] = jnp.where(rows == 0, 0.0, face)
            prev = jnp.where(lanes == 0, 0.0, pltpu.roll(x, 1, axis=1))
            succ = jnp.where(lanes == ap - 1, 0.0, pltpu.roll(x, ap - 1, axis=1))
            face = 0.5 * (x + prev)
            total = total + face + 0.5 * (x + succ)
            cc[d, c0 : c0 + CHUNK, :] = jnp.where(lanes == 0, 0.0, face)
            low = 0.5 * (x + jnp.where(first, 0.0, bz[d, at, :]))
            high = 0.5 * (x + jnp.where(last, 0.0, bz[d + 2, at, :]))
            fd[d, c0 : c0 + CHUNK, :] = jnp.where(first, 0.0, low)
            fd[d + 1, c0 : c0 + CHUNK, :] = jnp.where(last, 0.0, high)
            dg[d, c0 : c0 + CHUNK, :] = total + low + high

    def spread(field, d, c0):
        at = PAD + c0
        x = field[d + 1, at : at + CHUNK, :]
        across = cc[d, c0 : c0 + CHUNK, :]
        total = fd[d, c0 : c0 + CHUNK, :] * field[d, at : at + CHUNK, :]
        total = total + fd[d + 1, c0 : c0 + CHUNK, :] * field[d + 2, at : at + CHUNK, :]
        total = total + cr[d, at : at + CHUNK, :] * field[d + 1, at - 1 : at - 1 + CHUNK, :]
        total = total + cr[d, at + 1 : at + 1 + CHUNK, :] * field[d + 1, at + 1 : at + 1 + CHUNK, :]
        total = total + across * pltpu.roll(x, 1, axis=1)
        total = total + pltpu.roll(across * x, ap - 1, axis=1)
        return total - dg[d, c0 : c0 + CHUNK, :] * x, x

    def forward(n):
        def step(d):
            for c0 in range(0, ap, CHUNK):
                rows = slice(c0, c0 + CHUNK)
                at = slice(PAD + c0, PAD + c0 + CHUNK)
                q, x = spread(pb.at[n + 1], d, c0)
                qb[n, d, rows, :] = q
                nxt = 2.0 * x - pb[n, d + 1, at, :] + kp[d, rows, :] * q
                pb[n + 2, d + 1, at, :] = nxt + wavelet[0, n] * sf[d, rows, :]

        return step

    def backward(n):
        m = NT - n

        def step(d):
            for c0 in range(0, ap, CHUNK):
                rows = slice(c0, c0 + CHUNK)
                at = slice(PAD + c0, PAD + c0 + CHUNK)
                q, _ = spread(wb.at[m], d, c0)
                now = 2.0 * ab[m + 1, d, rows, :] - ab[m, d, rows, :] + q
                now = now + (kc[d, rows, :] * pb[n + 1, d + 1, at, :] - ob[n - 1, d, rows, :])
                ab[m + 2, d, rows, :] = now
                if n > 1:
                    wb[m + 1, d + 1, at, :] = kp[d, rows, :] * now
                term = now * qb[n - 1, d, rows, :]
                gb[d, rows, :] = term if m == 0 else gb[d, rows, :] + term

        return step

    groups = ((4, 8, 0), (2, 4, 8), (0, 2, 12))

    def slot_of(r, d):
        low, high, base = groups[r]
        upper = d // (depth // 2)
        return base + d - low - upper * (depth - 2 * high)

    def grad_copy(r, o, spot_rows):
        low, high, base = groups[r]
        places = pl.ds(base, 2 * (high - low))
        return remote(
            gc.at[places, spot_rows, :],
            gr.at[o, places],
            grad_send.at[r, o],
            grad_recv.at[r, o],
            half * 8 + peer(o),
            slab,
        )

    pieces = [[grad_copy(r, o, rows_of(peer(o))) for o in range(7)] for r in range(3)]
    merges = []
    for r, (low, high, base) in enumerate(groups):
        places = pl.ds(base, 2 * (high - low))
        merges.append(
            remote(
                acc.at[1 - half, places],
                pr.at[places],
                merge_send.at[r],
                merge_recv.at[r],
                partner,
                slab,
            )
        )

    def hand_in(r):
        low, high, _ = groups[r]

        def wind(d):
            gc[slot_of(r, d)] = unwind(gb[d], col_anchor % ap, ap - row_anchor)

        each(low, high, wind)
        for copy in pieces[r]:
            start_remote(copy)

    def collect(r):
        low, high, base = groups[r]
        for copy in pieces[r]:
            finish_of(copy)

        def one(t, carry):
            sums = [jnp.zeros((own, ap), f32) for _ in range(4)]
            for o in range(8):
                value = gr[o, t] if o < 7 else gc[t, home, :]
                member = half * 8 + (origin(o) if o < 7 else lane_group)
                keep_row = my_rows >= anchors[0, member]
                keep_col = my_lanes >= anchors[1, member]
                top = jnp.where(keep_row, value, 0.0)
                bottom = jnp.where(keep_row, 0.0, value)
                sums[0] += jnp.where(keep_col, top, 0.0)
                sums[1] += jnp.where(keep_col, 0.0, top)
                sums[2] += jnp.where(keep_col, bottom, 0.0)
                sums[3] += jnp.where(keep_col, 0.0, bottom)
            acc[0, t, :, :ap] = sums[0]
            acc[0, t, :, ap:] = sums[1]
            acc[1, t, :, :ap] = sums[2]
            acc[1, t, :, ap:] = sums[3]
            return carry

        lax.fori_loop(base, base + 2 * (high - low), one, 0)
        start_remote(merges[r])

    def finish(r):
        low, high, base = groups[r]
        finish_of(merges[r])

        def one(t, carry):
            pr[t] = pr[t] + acc[half, t]
            return carry

        lax.fori_loop(base, base + 2 * (high - low), one, 0)
        size = high - low
        for e in range(2):
            start_local(
                pltpu.make_async_copy(
                    pr.at[pl.ds(base + e * size, size)],
                    grad_out.at[pl.ds(low if e == 0 else depth - high, size)],
                    out_sem.at[4 + 2 * r + e],
                )
            )

    for i in range(2, 6):
        finish_of(loads[i])
    settle(0)
    go(buoy_halo)
    settle(1)
    arrived(buoy_halo)
    arrived(wave_halo[0])
    coefficients_first = 3
    each(0, coefficients_first, coefficients)
    each(0, 1, forward(0))
    go(wave_halo[1])
    each(1, 3, forward(0))
    go(back_halo[0])
    settle(2)
    each(3, 5, coefficients)
    each(3, 5, forward(0))
    arrived(wave_halo[1])
    each(0, 1, forward(1))
    go(wave_halo[2])
    each(1, 4, forward(1))
    settle(3)
    each(5, 8, coefficients)
    each(5, 8, forward(0))
    arrived(wave_halo[2])
    each(0, 1, forward(2))
    go(wave_halo[3])
    each(4, 8, forward(1))
    each(1, 8, forward(2))
    arrived(back_halo[0])
    arrived(wave_halo[3])
    each(0, 1, forward(3))
    each(0, 1, backward(4))
    go(back_halo[1])
    each(1, 8, forward(3))
    start_local(pltpu.make_async_copy(pb.at[NT, body, inner, :], wave_out.at[0, 0], out_sem.at[0]))
    start_local(pltpu.make_async_copy(pb.at[NT + 1, body, inner, :], wave_out.at[0, 1], out_sem.at[1]))
    each(1, 8, backward(4))
    each(2, 8, backward(3))
    each(3, 8, backward(2))
    each(4, 8, backward(1))
    hand_in(0)
    arrived(back_halo[1])
    each(0, 1, backward(3))
    go(back_halo[2])
    each(1, 2, backward(3))
    each(1, 3, backward(2))
    each(2, 4, backward(1))
    hand_in(1)
    arrived(back_halo[2])
    each(0, 1, backward(2))
    go(back_halo[3])
    start_local(pltpu.make_async_copy(ab.at[NT], adjoint_out.at[0, 0], out_sem.at[2]))
    each(1, 2, backward(1))
    collect(0)
    arrived(back_halo[3])
    each(0, 1, backward(1))
    hand_in(2)
    start_local(pltpu.make_async_copy(ab.at[NT + 1], adjoint_out.at[0, 1], out_sem.at[3]))
    collect(1)
    finish(0)
    collect(2)
    finish(1)
    finish(2)
    for wait in sent:
        wait()
    for _, wait in due:
        wait()


def shards(
    kappa,
    buoyancy,
    anchors,
    wave_start,
    adjoint_start,
    wavelet,
    source_cell,
    receiver_cells,
    observed,
):
    depth, own, side = kappa.shape
    ap = wave_start.shape[3]
    count = receiver_cells.shape[1]
    parts = depth // 4
    f32 = jnp.float32
    any_space = pl.BlockSpec(memory_space=pl.ANY)
    smem = pl.BlockSpec(memory_space=pltpu.SMEM)
    vmem = pl.BlockSpec(memory_space=pltpu.VMEM)
    padded = (depth + 2, ap + 2 * PAD, ap)
    plain = (depth, ap, ap)
    return pl.pallas_call(
        kernel,
        out_shape=(
            jax.ShapeDtypeStruct(kappa.shape, f32),
            jax.ShapeDtypeStruct(wave_start.shape, f32),
            jax.ShapeDtypeStruct(adjoint_start.shape, f32),
        ),
        in_specs=[smem, smem, smem, any_space, any_space, any_space, any_space, vmem, vmem],
        out_specs=(any_space, any_space, any_space),
        scratch_shapes=[
            pltpu.VMEM((2, 2, depth, own, side), f32),
            pltpu.VMEM((parts, 7, 2, 4, own, ap), f32),
            pltpu.VMEM((parts, 2, 4, ap, ap), f32),
            pltpu.VMEM((NT + 2,) + padded, f32),
            pltpu.VMEM((NT,) + plain, f32),
            pltpu.VMEM(plain, f32),
            pltpu.VMEM(padded, f32),
            pltpu.VMEM((depth + 1, ap, ap), f32),
            pltpu.VMEM((depth, ap + 2 * PAD, ap), f32),
            pltpu.VMEM(plain, f32),
            pltpu.VMEM(plain, f32),
            pltpu.VMEM((NT,) + padded, f32),
            pltpu.VMEM((NT + 2,) + plain, f32),
            pltpu.VMEM(plain, f32),
            pltpu.VMEM((NT,) + plain, f32),
            pltpu.VMEM(plain, f32),
            pltpu.VMEM((13 * ap, count), jnp.bfloat16),
            pltpu.VMEM(plain, f32),
            pltpu.VMEM(plain, f32),
            pltpu.VMEM((7, depth, own, ap), f32),
            pltpu.VMEM((2, depth, own, side), f32),
            pltpu.VMEM((depth, own, side), f32),
            pltpu.VMEM((2 * ap, ap), f32),
            pltpu.SemaphoreType.DMA((6,)),
            pltpu.SemaphoreType.DMA((parts, 2, 2)),
            pltpu.SemaphoreType.DMA((parts, 2, 2)),
            pltpu.SemaphoreType.DMA((parts, 7)),
            pltpu.SemaphoreType.DMA((parts, 7)),
            pltpu.SemaphoreType.DMA((2 * NT + 1, 2)),
            pltpu.SemaphoreType.DMA((2 * NT + 1, 2)),
            pltpu.SemaphoreType.DMA((3, 7)),
            pltpu.SemaphoreType.DMA((3, 7)),
            pltpu.SemaphoreType.DMA((3,)),
            pltpu.SemaphoreType.DMA((3,)),
            pltpu.SemaphoreType.DMA((10,)),
        ],
        compiler_params=pltpu.CompilerParams(
            collective_id=0, has_side_effects=True, vmem_limit_bytes=60 * 1024 * 1024
        ),
    )(
        anchors.T,
        wavelet,
        source_cell,
        kappa,
        buoyancy,
        wave_start,
        adjoint_start,
        jnp.transpose(receiver_cells, (2, 0, 1)),
        observed[0],
    )


def solution(mesh):
    in_specs = (
        P("slab", "shot", None),
        P("slab", "shot", None),
        P(),
        P("shot", None, "slab", None, None),
        P("shot", None, "slab", None, None),
        P("shot", None),
        P("shot", None),
        P("shot", None, None),
        P("shot", None, None),
    )
    out_specs = (
        P("slab", "shot", None),
        P("shot", None, "slab", None, None),
        P("shot", None, "slab", None, None),
    )
    return jax.shard_map(shards, mesh=mesh, in_specs=in_specs, out_specs=out_specs, check_vma=False)
```

time: 108 us -> 82.4 us (0.76)
  Pallas kernels: 96.7 us -> 74.3 us
  local copies, waits for them, and re-layouts: 8.92 us -> 6.28 us
    pallas_call x1, Pallas kernels: 96.7 us -> 74.3 us  [shards(): pl.pallas_call(kernel, out_shape=(jax.ShapeDtypeStruct(kappa.shape, f32),...]
    unnamed x7 -> x5, local copies, waits for them, and re-layouts: 8.92 us -> 6.28 us
where the time goes in v2:
time: 82.4 us; the launch traced here: 81.3 us
  Pallas kernels  74.3 us (90%)
  local copies, waits for them, and re-layouts  6.28 us (8%)
    pallas_call x1, Pallas kernels, shards(): pl.pallas_call(kernel, out_shape=(jax.ShapeDtypeStruct(kappa.shape, f32),...  74.3 us
    unnamed x5, local copies, waits for them, and re-layouts  6.28 us

profile of v2, /device:TPU:0, one launch (start us, length us, event | category | flops | bytes accessed | tf_op | source)
XLA Modules:
  0.0 81.3 jit_solution(13632014520687828858)
XLA Ops:
  0.6 74.3 %shard_map.112 = (f32[16,16,256]{2,1,0:T(8,128)}, f32[1,2,16,128,128]{4,3,2,1,0:T(8,128)}, f32[1,2,16,128,128]{4,3,2,1,0:T(8,128)}) custom-call(s32[2,16]{1,0:T(2,128)} %bitcast.5, f32[1,4]{1,0:T(1,128)} %wavelet.1, s32[1,3]{1,0:T(1,128)} %source.1, f32[16,16,256]{2,1,0:T(8,128)} %kappa.1, f32[16,16,256]{2,1,0:T(8,128)} %buoyancy.1, ...), custom_call_target="tpu_custom_call" | custom-call | tf_op jit(solution)/shard_map/pallas_call | solution.py:603
  75.0 1.7 %copy.15 = f32[16,16,256]{2,1,0:T(8,128)} copy(f32[16,16,256]{2,1,0:T(8,128)} %get-tuple-element.6) | data formatting | bytes 524288
  76.7 0.0 copy-start
  76.7 3.3 %copy.16 = f32[1,2,16,128,128]{4,3,2,1,0:T(8,128)} copy(f32[1,2,16,128,128]{4,3,2,1,0:T(8,128)} %get-tuple-element.7) | data formatting | bytes 4194304
  79.9 0.0 copy-done
  79.9 1.3 %copy.17 = f32[1,2,16,128,128]{4,3,2,1,0:T(8,128)} copy(f32[1,2,16,128,128]{4,3,2,1,0:T(8,128)S(1)} %copy-done) | data formatting | bytes 4194304
Async XLA Ops:
  76.7 3.3 %copy-start = (f32[1,2,16,128,128]{4,3,2,1,0:T(8,128)S(1)}, f32[1,2,16,128,128]{4,3,2,1,0:T(8,128)}, u32[]{:S(2)}) copy-start(f32[1,2,16,128,128]{4,3,2,1,0:T(8,128)} %get-tuple-element.8) | copy-start | bytes 6291460

commit v3 on v2

--- a/solution.py
+++ b/solution.py
@@ -9,6 +9,8 @@
 NT = 4
 PAD = 8
 CHUNK = 32
+PARTS = ((0, 1), (1, 3), (3, 5), (5, 8))
+RETURNS = ((4, 8), (2, 4), (1, 2), (0, 1))
 OFFSETS = ((2, 0), (2, 1), (1, 0), (3, 0), (1, 1), (3, 1), (0, 1))
 
 
@@ -74,7 +76,6 @@
     partner = (shot + 8) % 16
     below = (slab + 1) % slabs
     above = (slab + slabs - 1) % slabs
-    parts = depth // 4
 
     def peer(o):
         dx, dc = OFFSETS[o]
@@ -182,7 +183,7 @@
 
     lax.fori_loop(0, depth, mark, 0)
 
-    group = depth // parts
+    group = 4
 
     def spot(ch):
         at = lax.broadcasted_iota(jnp.int32, (group * ap, count), 0) + ch * (group * ap)
@@ -204,15 +205,21 @@
 
     pl.semaphore_wait(barrier, 10)
 
-    def plane_of(q, p):
-        return 2 * q + p + (p // 2) * (depth - 4 - 4 * q)
+    def plane_of(span, p):
+        low, high = span
+        width = high - low
+        return low + p + (p // width) * (depth - high - low - width)
+
+    def places_of(span):
+        low, high = span
+        return pl.ds(2 * low, 2 * (high - low))
 
     swaps = []
-    for q in range(parts):
+    for q, (low, high) in enumerate(PARTS):
         swaps.append([])
         for i, ref in enumerate((buoyancy, kappa)):
             for e in range(2):
-                planes = pl.ds(plane_of(q, 2 * e), 2)
+                planes = pl.ds(low if e == 0 else depth - high, high - low)
                 swaps[q].append(
                     remote(
                         ref.at[planes],
@@ -276,8 +283,8 @@
 
     def window_copy(q, o, spot_rows):
         return remote(
-            pack.at[q, o],
-            win.at[q, :, :, spot_rows, :],
+            pack.at[o, places_of(PARTS[q])],
+            win.at[places_of(PARTS[q]), :, spot_rows, :],
             win_send.at[q, o],
             win_recv.at[q, o],
             half * 8 + peer(o),
@@ -286,12 +293,13 @@
 
     finish_of(loads[0])
     finish_of(loads[1])
-    for q in range(parts):
+    for q, part in enumerate(PARTS):
         for copy in swaps[q]:
             finish_of(copy)
 
         def fill(p, carry):
-            d = plane_of(q, p)
+            d = plane_of(part, p)
+            t = 2 * part[0] + p
             for i in range(2):
                 low = raw[0, i, d]
                 high = raw[1, i, d]
@@ -303,133 +311,162 @@
                     b = jnp.where(keep_col, high[:, :ap], high[:, ap:])
                     value = jnp.where(keep_row, a, b)
                     if o < 7:
-                        pack[q, o, i, p] = value
+                        pack[o, t, i] = value
                     else:
-                        win[q, i, p, home, :] = value
+                        win[t, i, home, :] = value
             return carry
 
-        lax.fori_loop(0, 4, fill, 0)
+        lax.fori_loop(0, 2 * (part[1] - part[0]), fill, 0)
         for o in range(7):
             copy = window_copy(q, o, home)
             copy.start()
             sent.append(copy.wait_send)
             landing = window_copy(q, o, rows_of(origin(o)))
             due.append(((q, o), landing.wait_recv))
-        if q + 2 < parts:
+        if q + 2 < len(PARTS):
             swap_part(q + 2)
-        elif q + 2 == parts:
+        elif q + 2 == len(PARTS):
             go(wave_halo[0])
         spot(q)
 
     row_anchor = anchors[0, shot]
     col_anchor = anchors[1, shot]
 
-    def unwind(x, lane_shift, first_row):
-        x = pltpu.roll(x, lane_shift, axis=1)
-        tmp[:ap, :] = x
-        tmp[ap:, :] = x
-        return tmp[pl.ds(first_row, ap), :]
+    def unwind(values, lane_shift, first_row):
+        for t, x in enumerate(values):
+            x = pltpu.roll(x, lane_shift, axis=1)
+            tmp[t, :ap, :] = x
+            tmp[t, ap:, :] = x
+        return [tmp[t, pl.ds(first_row, ap), :] for t in range(len(values))]
 
     lane_back = (ap - col_anchor) % ap
 
     def settle(q):
+        low, high = PARTS[q]
+        width = high - low
         for o in range(7):
             finish_of((q, o))
 
         def one(p, carry):
-            d = plane_of(q, p)
-            bz[d + 1, inner, :] = unwind(win[q, 0, p], lane_back, row_anchor)
-            k = unwind(win[q, 1, p], lane_back, row_anchor)
-            kp[d] = k
-            wb[0, d + 1, inner, :] = k * ab[1, d]
+            t = 2 * low + p
+            values = [win[t, 0], win[t, 1], win[t + width, 0], win[t + width, 1]]
+            values = unwind(values, lane_back, row_anchor)
+            products = []
+            for e in range(2):
+                d = low + p if e == 0 else depth - high + p
+                products.append(values[2 * e + 1] * ab[1, d])
+            for e in range(2):
+                d = low + p if e == 0 else depth - high + p
+                bz[d + 1, inner, :] = values[2 * e]
+                kp[d] = values[2 * e + 1]
+                wb[0, d + 1, inner, :] = products[e]
             return carry
 
-        lax.fori_loop(0, 4, one, 0)
+        lax.fori_loop(0, width, one, 0)
 
     def each(low, high, step):
-        def both(i, carry):
-            d = low + i // 2
-            step(d + (i % 2) * (depth - 1 - 2 * d))
+        pairs = 2 if (high - low) % 2 == 0 else 1
+
+        def some(i, carry):
+            layers = []
+            for t in range(pairs):
+                d = low + i * pairs + t
+                layers += [d, depth - 1 - d]
+            for c0 in range(0, ap, CHUNK):
+                stores = [step(d, c0) for d in layers]
+                for store in stores:
+                    store()
             return carry
 
-        lax.fori_loop(0, 2 * (high - low), both, 0)
-
-    def coefficients(d):
+        lax.fori_loop(0, (high - low) // pairs, some, 0)
+
+    def coefficients(d, c0):
         first = (slab == 0) & (d == 0)
         last = (slab == slabs - 1) & (d == depth - 1)
-        for c0 in range(0, ap, CHUNK):
-            rows = lax.broadcasted_iota(jnp.int32, (CHUNK, ap), 0) + c0
-            lanes = lax.broadcasted_iota(jnp.int32, (CHUNK, ap), 1)
-            at = slice(PAD + c0, PAD + c0 + CHUNK)
-            x = bz[d + 1, at, :]
-            prev = bz[d + 1, PAD + c0 - 1 : PAD + c0 - 1 + CHUNK, :]
-            succ = bz[d + 1, PAD + c0 + 1 : PAD + c0 + 1 + CHUNK, :]
-            face = 0.5 * (x + prev)
-            total = face + 0.5 * (x + succ)
-            cr[d, at, :] = jnp.where(rows == 0, 0.0, face)
-            prev = jnp.where(lanes == 0, 0.0, pltpu.roll(x, 1, axis=1))
-            succ = jnp.where(lanes == ap - 1, 0.0, pltpu.roll(x, ap - 1, axis=1))
-            face = 0.5 * (x + prev)
-            total = total + face + 0.5 * (x + succ)
-            cc[d, c0 : c0 + CHUNK, :] = jnp.where(lanes == 0, 0.0, face)
-            low = 0.5 * (x + jnp.where(first, 0.0, bz[d, at, :]))
-            high = 0.5 * (x + jnp.where(last, 0.0, bz[d + 2, at, :]))
-            fd[d, c0 : c0 + CHUNK, :] = jnp.where(first, 0.0, low)
-            fd[d + 1, c0 : c0 + CHUNK, :] = jnp.where(last, 0.0, high)
-            dg[d, c0 : c0 + CHUNK, :] = total + low + high
+        rows = lax.broadcasted_iota(jnp.int32, (CHUNK, ap), 0) + c0
+        lanes = lax.broadcasted_iota(jnp.int32, (CHUNK, ap), 1)
+        at = slice(PAD + c0, PAD + c0 + CHUNK)
+        x = bz[d + 1, at, :]
+        prev = bz[d + 1, PAD + c0 - 1 : PAD + c0 - 1 + CHUNK, :]
+        succ = bz[d + 1, PAD + c0 + 1 : PAD + c0 + 1 + CHUNK, :]
+        across = 0.5 * (x + prev)
+        total = across + 0.5 * (x + succ)
+        across = jnp.where(rows == 0, 0.0, across)
+        prev = jnp.where(lanes == 0, 0.0, pltpu.roll(x, 1, axis=1))
+        succ = jnp.where(lanes == ap - 1, 0.0, pltpu.roll(x, ap - 1, axis=1))
+        along = 0.5 * (x + prev)
+        total = total + along + 0.5 * (x + succ)
+        along = jnp.where(lanes == 0, 0.0, along)
+        low = 0.5 * (x + jnp.where(first, 0.0, bz[d, at, :]))
+        high = 0.5 * (x + jnp.where(last, 0.0, bz[d + 2, at, :]))
+        total = total + low + high
+        low = jnp.where(first, 0.0, low)
+        high = jnp.where(last, 0.0, high)
+
+        def store():
+            cr[d, at, :] = across
+            cc[d, c0 : c0 + CHUNK, :] = along
+            fd[d, c0 : c0 + CHUNK, :] = low
+            fd[d + 1, c0 : c0 + CHUNK, :] = high
+            dg[d, c0 : c0 + CHUNK, :] = total
+
+        return store
 
     def spread(field, d, c0):
         at = PAD + c0
         x = field[d + 1, at : at + CHUNK, :]
         across = cc[d, c0 : c0 + CHUNK, :]
+        sides = across * pltpu.roll(x, 1, axis=1)
+        sides = sides + pltpu.roll(across * x, ap - 1, axis=1)
         total = fd[d, c0 : c0 + CHUNK, :] * field[d, at : at + CHUNK, :]
         total = total + fd[d + 1, c0 : c0 + CHUNK, :] * field[d + 2, at : at + CHUNK, :]
         total = total + cr[d, at : at + CHUNK, :] * field[d + 1, at - 1 : at - 1 + CHUNK, :]
         total = total + cr[d, at + 1 : at + 1 + CHUNK, :] * field[d + 1, at + 1 : at + 1 + CHUNK, :]
-        total = total + across * pltpu.roll(x, 1, axis=1)
-        total = total + pltpu.roll(across * x, ap - 1, axis=1)
-        return total - dg[d, c0 : c0 + CHUNK, :] * x, x
+        return (total - dg[d, c0 : c0 + CHUNK, :] * x) + sides, x
 
     def forward(n):
-        def step(d):
-            for c0 in range(0, ap, CHUNK):
-                rows = slice(c0, c0 + CHUNK)
-                at = slice(PAD + c0, PAD + c0 + CHUNK)
-                q, x = spread(pb.at[n + 1], d, c0)
+        def step(d, c0):
+            rows = slice(c0, c0 + CHUNK)
+            at = slice(PAD + c0, PAD + c0 + CHUNK)
+            q, x = spread(pb.at[n + 1], d, c0)
+            nxt = 2.0 * x - pb[n, d + 1, at, :] + wavelet[0, n] * sf[d, rows, :]
+            nxt = nxt + kp[d, rows, :] * q
+
+            def store():
                 qb[n, d, rows, :] = q
-                nxt = 2.0 * x - pb[n, d + 1, at, :] + kp[d, rows, :] * q
-                pb[n + 2, d + 1, at, :] = nxt + wavelet[0, n] * sf[d, rows, :]
+                pb[n + 2, d + 1, at, :] = nxt
+
+            return store
 
         return step
 
     def backward(n):
         m = NT - n
 
-        def step(d):
-            for c0 in range(0, ap, CHUNK):
-                rows = slice(c0, c0 + CHUNK)
-                at = slice(PAD + c0, PAD + c0 + CHUNK)
-                q, _ = spread(wb.at[m], d, c0)
-                now = 2.0 * ab[m + 1, d, rows, :] - ab[m, d, rows, :] + q
-                now = now + (kc[d, rows, :] * pb[n + 1, d + 1, at, :] - ob[n - 1, d, rows, :])
+        def step(d, c0):
+            rows = slice(c0, c0 + CHUNK)
+            at = slice(PAD + c0, PAD + c0 + CHUNK)
+            q, _ = spread(wb.at[m], d, c0)
+            now = 2.0 * ab[m + 1, d, rows, :] - ab[m, d, rows, :]
+            now = now + (kc[d, rows, :] * pb[n + 1, d + 1, at, :] - ob[n - 1, d, rows, :])
+            now = now + q
+            product = kp[d, rows, :] * now if n > 1 else None
+            term = now * qb[n - 1, d, rows, :]
+            if m > 0:
+                term = gb[d, rows, :] + term
+
+            def store():
                 ab[m + 2, d, rows, :] = now
                 if n > 1:
-                    wb[m + 1, d + 1, at, :] = kp[d, rows, :] * now
-                term = now * qb[n - 1, d, rows, :]
-                gb[d, rows, :] = term if m == 0 else gb[d, rows, :] + term
+                    wb[m + 1, d + 1, at, :] = product
+                gb[d, rows, :] = term
+
+            return store
 
         return step
 
-    groups = ((4, 8, 0), (2, 4, 8), (0, 2, 12))
-
-    def slot_of(r, d):
-        low, high, base = groups[r]
-        upper = d // (depth // 2)
-        return base + d - low - upper * (depth - 2 * high)
-
     def grad_copy(r, o, spot_rows):
-        low, high, base = groups[r]
-        places = pl.ds(base, 2 * (high - low))
+        places = places_of(RETURNS[r])
         return remote(
             gc.at[places, spot_rows, :],
             gr.at[o, places],
@@ -439,10 +476,10 @@
             slab,
         )
 
-    pieces = [[grad_copy(r, o, rows_of(peer(o))) for o in range(7)] for r in range(3)]
+    pieces = [[grad_copy(r, o, rows_of(peer(o))) for o in range(7)] for r in range(len(RETURNS))]
     merges = []
-    for r, (low, high, base) in enumerate(groups):
-        places = pl.ds(base, 2 * (high - low))
+    for r, span in enumerate(RETURNS):
+        places = places_of(span)
         merges.append(
             remote(
                 acc.at[1 - half, places],
@@ -455,17 +492,21 @@
         )
 
     def hand_in(r):
-        low, high, _ = groups[r]
-
-        def wind(d):
-            gc[slot_of(r, d)] = unwind(gb[d], col_anchor % ap, ap - row_anchor)
-
-        each(low, high, wind)
+        low, high = RETURNS[r]
+        width = high - low
+
+        def wind(p, carry):
+            values = unwind([gb[low + p], gb[depth - high + p]], col_anchor % ap, ap - row_anchor)
+            gc[2 * low + p] = values[0]
+            gc[2 * low + width + p] = values[1]
+            return carry
+
+        lax.fori_loop(0, width, wind, 0)
         for copy in pieces[r]:
             start_remote(copy)
 
     def collect(r):
-        low, high, base = groups[r]
+        low, high = RETURNS[r]
         for copy in pieces[r]:
             finish_of(copy)
 
@@ -488,23 +529,23 @@
             acc[1, t, :, ap:] = sums[3]
             return carry
 
-        lax.fori_loop(base, base + 2 * (high - low), one, 0)
+        lax.fori_loop(2 * low, 2 * high, one, 0)
         start_remote(merges[r])
 
     def finish(r):
-        low, high, base = groups[r]
+        low, high = RETURNS[r]
         finish_of(merges[r])
 
         def one(t, carry):
             pr[t] = pr[t] + acc[half, t]
             return carry
 
-        lax.fori_loop(base, base + 2 * (high - low), one, 0)
+        lax.fori_loop(2 * low, 2 * high, one, 0)
         size = high - low
         for e in range(2):
             start_local(
                 pltpu.make_async_copy(
-                    pr.at[pl.ds(base + e * size, size)],
+                    pr.at[pl.ds(2 * low + e * size, size)],
                     grad_out.at[pl.ds(low if e == 0 else depth - high, size)],
                     out_sem.at[4 + 2 * r + e],
                 )
@@ -517,45 +558,48 @@
     settle(1)
     arrived(buoy_halo)
     arrived(wave_halo[0])
-    coefficients_first = 3
-    each(0, coefficients_first, coefficients)
+    each(0, 2, coefficients)
     each(0, 1, forward(0))
     go(wave_halo[1])
-    each(1, 3, forward(0))
+    each(1, 2, forward(0))
     go(back_halo[0])
-    settle(2)
-    each(3, 5, coefficients)
-    each(3, 5, forward(0))
     arrived(wave_halo[1])
     each(0, 1, forward(1))
     go(wave_halo[2])
-    each(1, 4, forward(1))
-    settle(3)
-    each(5, 8, coefficients)
-    each(5, 8, forward(0))
+    settle(2)
+    each(2, 4, coefficients)
+    each(2, 4, forward(0))
+    each(1, 3, forward(1))
     arrived(wave_halo[2])
     each(0, 1, forward(2))
     go(wave_halo[3])
-    each(4, 8, forward(1))
-    each(1, 8, forward(2))
+    each(1, 2, forward(2))
     arrived(back_halo[0])
     arrived(wave_halo[3])
     each(0, 1, forward(3))
     each(0, 1, backward(4))
     go(back_halo[1])
-    each(1, 8, forward(3))
+    settle(3)
+    each(4, 8, coefficients)
+    each(4, 8, forward(0))
+    each(3, 4, forward(1))
+    each(4, 8, forward(1))
+    each(2, 8, forward(2))
+    each(1, 2, forward(3))
+    each(2, 8, forward(3))
     start_local(pltpu.make_async_copy(pb.at[NT, body, inner, :], wave_out.at[0, 0], out_sem.at[0]))
     start_local(pltpu.make_async_copy(pb.at[NT + 1, body, inner, :], wave_out.at[0, 1], out_sem.at[1]))
-    each(1, 8, backward(4))
-    each(2, 8, backward(3))
-    each(3, 8, backward(2))
-    each(4, 8, backward(1))
-    hand_in(0)
+    each(1, 2, backward(4))
+    each(2, 8, backward(4))
     arrived(back_halo[1])
     each(0, 1, backward(3))
     go(back_halo[2])
     each(1, 2, backward(3))
-    each(1, 3, backward(2))
+    each(2, 8, backward(3))
+    each(1, 2, backward(2))
+    each(2, 8, backward(2))
+    each(4, 8, backward(1))
+    hand_in(0)
     each(2, 4, backward(1))
     hand_in(1)
     arrived(back_halo[2])
@@ -563,16 +607,19 @@
     go(back_halo[3])
     start_local(pltpu.make_async_copy(ab.at[NT], adjoint_out.at[0, 0], out_sem.at[2]))
     each(1, 2, backward(1))
-    collect(0)
+    hand_in(2)
     arrived(back_halo[3])
     each(0, 1, backward(1))
-    hand_in(2)
+    hand_in(3)
     start_local(pltpu.make_async_copy(ab.at[NT + 1], adjoint_out.at[0, 1], out_sem.at[3]))
+    collect(0)
     collect(1)
+    collect(2)
     finish(0)
-    collect(2)
+    collect(3)
     finish(1)
     finish(2)
+    finish(3)
     for wait in sent:
         wait()
     for _, wait in due:
@@ -593,7 +640,7 @@
     depth, own, side = kappa.shape
     ap = wave_start.shape[3]
     count = receiver_cells.shape[1]
-    parts = depth // 4
+    parts = len(PARTS)
     f32 = jnp.float32
     any_space = pl.BlockSpec(memory_space=pl.ANY)
     smem = pl.BlockSpec(memory_space=pltpu.SMEM)
@@ -611,8 +658,8 @@
         out_specs=(any_space, any_space, any_space),
         scratch_shapes=[
             pltpu.VMEM((2, 2, depth, own, side), f32),
-            pltpu.VMEM((parts, 7, 2, 4, own, ap), f32),
-            pltpu.VMEM((parts, 2, 4, ap, ap), f32),
+            pltpu.VMEM((7, depth, 2, own, ap), f32),
+            pltpu.VMEM((depth, 2, ap, ap), f32),
             pltpu.VMEM((NT + 2,) + padded, f32),
             pltpu.VMEM((NT,) + plain, f32),
             pltpu.VMEM(plain, f32),
@@ -632,7 +679,7 @@
             pltpu.VMEM((7, depth, own, ap), f32),
             pltpu.VMEM((2, depth, own, side), f32),
             pltpu.VMEM((depth, own, side), f32),
-            pltpu.VMEM((2 * ap, ap), f32),
+            pltpu.VMEM((4, 2 * ap, ap), f32),
             pltpu.SemaphoreType.DMA((6,)),
             pltpu.SemaphoreType.DMA((parts, 2, 2)),
             pltpu.SemaphoreType.DMA((parts, 2, 2)),
@@ -640,11 +687,11 @@
             pltpu.SemaphoreType.DMA((parts, 7)),
             pltpu.SemaphoreType.DMA((2 * NT + 1, 2)),
             pltpu.SemaphoreType.DMA((2 * NT + 1, 2)),
-            pltpu.SemaphoreType.DMA((3, 7)),
-            pltpu.SemaphoreType.DMA((3, 7)),
-            pltpu.SemaphoreType.DMA((3,)),
-            pltpu.SemaphoreType.DMA((3,)),
-            pltpu.SemaphoreType.DMA((10,)),
+            pltpu.SemaphoreType.DMA((len(RETURNS), 7)),
+            pltpu.SemaphoreType.DMA((len(RETURNS), 7)),
+            pltpu.SemaphoreType.DMA((len(RETURNS),)),
+            pltpu.SemaphoreType.DMA((len(RETURNS),)),
+            pltpu.SemaphoreType.DMA((4 + 2 * len(RETURNS),)),
         ],
         compiler_params=pltpu.CompilerParams(
             collective_id=0, has_side_effects=True, vmem_limit_bytes=60 * 1024 * 1024

time: 82.4 us -> 83.3 us (1.011); the launches traced: 81.3 us -> 83.1 us
  Pallas kernels: 74.3 us -> 76.2 us
    pallas_call x1, Pallas kernels: 74.3 us -> 76.2 us  [shards(): pl.pallas_call(kernel, out_shape=(jax.ShapeDtypeStruct(kappa.shape, f32),...]
where the time goes in v3:
time: 83.3 us; the launch traced here: 83.1 us
  Pallas kernels  76.2 us (91%)
  local copies, waits for them, and re-layouts  6.28 us (8%)
    pallas_call x1, Pallas kernels, shards(): pl.pallas_call(kernel, out_shape=(jax.ShapeDtypeStruct(kappa.shape, f32),...  76.2 us
    unnamed x5, local copies, waits for them, and re-layouts  6.28 us

profile of v3, /device:TPU:0, one launch (start us, length us, event | category | flops | bytes accessed | tf_op | source)
XLA Modules:
  0.0 83.1 jit_solution(3080670175425910516)
XLA Ops:
  0.6 76.2 %shard_map.112 = (f32[16,16,256]{2,1,0:T(8,128)}, f32[1,2,16,128,128]{4,3,2,1,0:T(8,128)}, f32[1,2,16,128,128]{4,3,2,1,0:T(8,128)}) custom-call(s32[2,16]{1,0:T(2,128)} %bitcast.5, f32[1,4]{1,0:T(1,128)} %wavelet.1, s32[1,3]{1,0:T(1,128)} %source.1, f32[16,16,256]{2,1,0:T(8,128)} %kappa.1, f32[16,16,256]{2,1,0:T(8,128)} %buoyancy.1, ...), custom_call_target="tpu_custom_call" | custom-call | tf_op jit(solution)/shard_map/pallas_call | solution.py:650
  76.8 1.7 %copy.15 = f32[16,16,256]{2,1,0:T(8,128)} copy(f32[16,16,256]{2,1,0:T(8,128)} %get-tuple-element.6) | data formatting | bytes 524288
  78.5 0.0 copy-start
  78.5 3.3 %copy.16 = f32[1,2,16,128,128]{4,3,2,1,0:T(8,128)} copy(f32[1,2,16,128,128]{4,3,2,1,0:T(8,128)} %get-tuple-element.7) | data formatting | bytes 4194304
  81.8 0.0 copy-done
  81.8 1.3 %copy.17 = f32[1,2,16,128,128]{4,3,2,1,0:T(8,128)} copy(f32[1,2,16,128,128]{4,3,2,1,0:T(8,128)S(1)} %copy-done) | data formatting | bytes 4194304
Async XLA Ops:
  78.5 3.3 %copy-start = (f32[1,2,16,128,128]{4,3,2,1,0:T(8,128)S(1)}, f32[1,2,16,128,128]{4,3,2,1,0:T(8,128)}, u32[]{:S(2)}) copy-start(f32[1,2,16,128,128]{4,3,2,1,0:T(8,128)} %get-tuple-element.8) | copy-start | bytes 6291460

commit v4 on v3

--- a/solution.py
+++ b/solution.py
@@ -8,7 +8,7 @@
 MESH = pl.DeviceIdType.MESH
 NT = 4
 PAD = 8
-CHUNK = 32
+CHUNK = 128
 PARTS = ((0, 1), (1, 3), (3, 5), (5, 8))
 RETURNS = ((4, 8), (2, 4), (1, 2), (0, 1))
 OFFSETS = ((2, 0), (2, 1), (1, 0), (3, 0), (1, 1), (3, 1), (0, 1))
@@ -161,19 +161,19 @@
     rows_at = lax.broadcasted_iota(jnp.int32, (ap, ap), 0)
     lanes_at = lax.broadcasted_iota(jnp.int32, (ap, ap), 1)
     flat = (cells[0] - slab * depth) * ap + cells[1]
-    hit = cells[2] == lax.broadcasted_iota(jnp.int32, (ap, count), 0)
-
-    def place(row, values):
-        vb[row : row + ap, :] = jnp.where(hit, values, 0.0).astype(jnp.bfloat16)
+    upright = jnp.concatenate(
+        [cells[2].astype(f32), observed[...], jnp.zeros((7 - NT, count), f32)], axis=0
+    ).T
+    hit = lax.broadcasted_iota(jnp.int32, (count, ap), 1).astype(f32) == upright[:, :1]
 
     for n in range(NT):
-        rest = observed[n : n + 1, :]
+        rest = jnp.where(hit, upright[:, n + 1 : n + 2], 0.0)
         base = (n // 2) * 6 * ap + (n % 2) * ap
         for part in range(3):
-            top = rest.astype(jnp.bfloat16).astype(f32)
-            place(base + part * 2 * ap, top)
-            rest = rest - top
-    place(12 * ap, jnp.ones((1, count), f32))
+            top = rest.astype(jnp.bfloat16)
+            vb[:, base + part * 2 * ap : base + (part * 2 + 1) * ap] = top
+            rest = rest - top.astype(f32)
+    vb[:, 12 * ap :] = jnp.where(hit, 1.0, 0.0).astype(jnp.bfloat16)
 
     def mark(d, carry):
         here = (rows_at == source[0, 1]) & (lanes_at == source[0, 2])
@@ -191,7 +191,7 @@
 
         def times(row, width):
             return lax.dot_general(
-                onehot, vb[row : row + width, :], (((1,), (1,)), ((), ())), preferred_element_type=f32
+                onehot, vb[:, row : row + width], (((1,), (0,)), ((), ())), preferred_element_type=f32
             )
 
         for pair in range(NT // 2):
@@ -203,6 +203,8 @@
             ob[2 * pair + 1, pl.ds(ch * group, group), :, :] = total[:, :, ap:]
         kc[pl.ds(ch * group, group), :, :] = times(12 * ap, ap).reshape(group, ap, ap)
 
+    for ch in range(depth // group):
+        spot(ch)
     pl.semaphore_wait(barrier, 10)
 
     def plane_of(span, p):
@@ -293,7 +295,8 @@
 
     finish_of(loads[0])
     finish_of(loads[1])
-    for q, part in enumerate(PARTS):
+    def pack_part(q):
+        part = PARTS[q]
         for copy in swaps[q]:
             finish_of(copy)
 
@@ -317,17 +320,18 @@
             return carry
 
         lax.fori_loop(0, 2 * (part[1] - part[0]), fill, 0)
+
+    def send_part(q):
         for o in range(7):
             copy = window_copy(q, o, home)
             copy.start()
-            sent.append(copy.wait_send)
+            due.append(((q, o, "sent"), copy.wait_send))
             landing = window_copy(q, o, rows_of(origin(o)))
             due.append(((q, o), landing.wait_recv))
-        if q + 2 < len(PARTS):
-            swap_part(q + 2)
-        elif q + 2 == len(PARTS):
-            go(wave_halo[0])
-        spot(q)
+
+    def sent_part(q):
+        for o in range(7):
+            finish_of((q, o, "sent"))
 
     row_anchor = anchors[0, shot]
     col_anchor = anchors[1, shot]
@@ -551,13 +555,25 @@
                 )
             )
 
+    pack_part(0)
+    send_part(0)
+    swap_part(2)
+    pack_part(1)
+    send_part(1)
+    swap_part(3)
+    go(wave_halo[0])
+    pack_part(2)
+    send_part(2)
     for i in range(2, 6):
         finish_of(loads[i])
     settle(0)
     go(buoy_halo)
+    pack_part(3)
+    sent_part(1)
+    send_part(3)
+    arrived(wave_halo[0])
     settle(1)
     arrived(buoy_halo)
-    arrived(wave_halo[0])
     each(0, 2, coefficients)
     each(0, 1, forward(0))
     go(wave_halo[1])
@@ -574,26 +590,27 @@
     each(0, 1, forward(2))
     go(wave_halo[3])
     each(1, 2, forward(2))
+    settle(3)
+    each(4, 8, coefficients)
     arrived(back_halo[0])
     arrived(wave_halo[3])
     each(0, 1, forward(3))
     each(0, 1, backward(4))
     go(back_halo[1])
-    settle(3)
-    each(4, 8, coefficients)
     each(4, 8, forward(0))
     each(3, 4, forward(1))
     each(4, 8, forward(1))
-    each(2, 8, forward(2))
+    each(2, 4, forward(2))
+    each(4, 8, forward(2))
     each(1, 2, forward(3))
+    each(1, 2, backward(4))
     each(2, 8, forward(3))
     start_local(pltpu.make_async_copy(pb.at[NT, body, inner, :], wave_out.at[0, 0], out_sem.at[0]))
     start_local(pltpu.make_async_copy(pb.at[NT + 1, body, inner, :], wave_out.at[0, 1], out_sem.at[1]))
-    each(1, 2, backward(4))
-    each(2, 8, backward(4))
     arrived(back_halo[1])
     each(0, 1, backward(3))
     go(back_halo[2])
+    each(2, 8, backward(4))
     each(1, 2, backward(3))
     each(2, 8, backward(3))
     each(1, 2, backward(2))
@@ -626,6 +643,17 @@
         wait()
 
 
+def deliver(grad, wave, adjoint, grad_out, wave_out, adjoint_out, sem):
+    copies = [pltpu.make_async_copy(grad, grad_out, sem.at[0])]
+    for e in range(2):
+        copies.append(pltpu.make_async_copy(wave.at[0, e], wave_out.at[0, e], sem.at[1 + e]))
+        copies.append(pltpu.make_async_copy(adjoint.at[0, e], adjoint_out.at[0, e], sem.at[3 + e]))
+    for copy in copies:
+        copy.start()
+    for copy in copies:
+        copy.wait()
+
+
 def shards(
     kappa,
     buoyancy,
@@ -647,12 +675,12 @@
     vmem = pl.BlockSpec(memory_space=pltpu.VMEM)
     padded = (depth + 2, ap + 2 * PAD, ap)
     plain = (depth, ap, ap)
-    return pl.pallas_call(
+    results = pl.pallas_call(
         kernel,
         out_shape=(
-            jax.ShapeDtypeStruct(kappa.shape, f32),
-            jax.ShapeDtypeStruct(wave_start.shape, f32),
-            jax.ShapeDtypeStruct(adjoint_start.shape, f32),
+            pltpu.VMEM(kappa.shape, f32),
+            pltpu.VMEM(wave_start.shape, f32),
+            pltpu.VMEM(adjoint_start.shape, f32),
         ),
         in_specs=[smem, smem, smem, any_space, any_space, any_space, any_space, vmem, vmem],
         out_specs=(any_space, any_space, any_space),
@@ -673,7 +701,7 @@
             pltpu.VMEM(plain, f32),
             pltpu.VMEM((NT,) + plain, f32),
             pltpu.VMEM(plain, f32),
-            pltpu.VMEM((13 * ap, count), jnp.bfloat16),
+            pltpu.VMEM((count, 13 * ap), jnp.bfloat16),
             pltpu.VMEM(plain, f32),
             pltpu.VMEM(plain, f32),
             pltpu.VMEM((7, depth, own, ap), f32),
@@ -694,7 +722,7 @@
             pltpu.SemaphoreType.DMA((4 + 2 * len(RETURNS),)),
         ],
         compiler_params=pltpu.CompilerParams(
-            collective_id=0, has_side_effects=True, vmem_limit_bytes=60 * 1024 * 1024
+            collective_id=0, has_side_effects=True, vmem_limit_bytes=57 * 1024 * 1024
         ),
     )(
         anchors.T,
@@ -707,6 +735,7 @@
         jnp.transpose(receiver_cells, (2, 0, 1)),
         observed[0],
     )
+    return results
 
 
 def solution(mesh):

time: 83.3 us -> 78 us (0.936)
  local copies, waits for them, and re-layouts: 6.28 us -> 3.34 us
  Pallas kernels: 76.2 us -> 73.9 us
    unnamed x5 -> x3, local copies, waits for them, and re-layouts: 6.28 us -> 3.34 us
    pallas_call x1, Pallas kernels: 76.2 us -> 73.9 us  [shards(): pl.pallas_call(kernel, out_shape=(pltpu.VMEM(kappa.shape, f32), pltpu.VME...]
where the time goes in v4:
time: 78 us; the launch traced here: 77.9 us
  Pallas kernels  73.9 us (95%)
  local copies, waits for them, and re-layouts  3.34 us (4%)
    pallas_call x1, Pallas kernels, shards(): pl.pallas_call(kernel, out_shape=(pltpu.VMEM(kappa.shape, f32), pltpu.VME...  73.9 us
    unnamed x3, local copies, waits for them, and re-layouts  3.34 us

profile of v4, /device:TPU:0, one launch (start us, length us, event | category | flops | bytes accessed | tf_op | source)
XLA Modules:
  0.0 77.9 jit_solution(3605989063598563208)
XLA Ops:
  0.6 73.9 %shard_map.112 = (f32[16,16,256]{2,1,0:T(8,128)S(1)}, f32[1,2,16,128,128]{4,3,2,1,0:T(8,128)S(1)}, f32[1,2,16,128,128]{4,3,2,1,0:T(8,128)S(1)}) custom-call(s32[2,16]{1,0:T(2,128)} %bitcast.5, f32[1,4]{1,0:T(1,128)} %wavelet.1, s32[1,3]{1,0:T(1,128)} %source.1, f32[16,16,256]{2,1,0:T(8,128)} %kappa.1, f32[16,16,256]{2,1,0:T(8,128)} %buoyancy.1, ...), custom_call_target="tpu_custom_call" | custom-call | tf_op jit(solution)/shard_map/pallas_call | solution.py:678
  74.6 0.7 copy.15
  75.3 1.3 %copy.16 = f32[1,2,16,128,128]{4,3,2,1,0:T(8,128)} copy(f32[1,2,16,128,128]{4,3,2,1,0:T(8,128)S(1)} %get-tuple-element.4) | data formatting | bytes 4194304
  76.6 1.3 %copy.17 = f32[1,2,16,128,128]{4,3,2,1,0:T(8,128)} copy(f32[1,2,16,128,128]{4,3,2,1,0:T(8,128)S(1)} %get-tuple-element.5) | data formatting | bytes 4194304

commit v5 on v4

--- a/solution.py
+++ b/solution.py
@@ -203,8 +203,6 @@
             ob[2 * pair + 1, pl.ds(ch * group, group), :, :] = total[:, :, ap:]
         kc[pl.ds(ch * group, group), :, :] = times(12 * ap, ap).reshape(group, ap, ap)
 
-    for ch in range(depth // group):
-        spot(ch)
     pl.semaphore_wait(barrier, 10)
 
     def plane_of(span, p):
@@ -273,7 +271,10 @@
         finish_of(pair[1])
 
     swap_part(0)
+    spot(0)
     swap_part(1)
+    for ch in range(1, depth // group):
+        spot(ch)
 
     my_rows = lax.broadcasted_iota(jnp.int32, (own, ap), 0) + lane_group * own
     my_lanes = lax.broadcasted_iota(jnp.int32, (own, ap), 1)
@@ -538,22 +539,17 @@
 
     def finish(r):
         low, high = RETURNS[r]
+        width = high - low
         finish_of(merges[r])
 
-        def one(t, carry):
-            pr[t] = pr[t] + acc[half, t]
+        def one(p, carry):
+            t = 2 * low + p
+            sums = [pr[t] + acc[half, t], pr[t + width] + acc[half, t + width]]
+            grad_out[low + p] = sums[0]
+            grad_out[depth - high + p] = sums[1]
             return carry
 
-        lax.fori_loop(2 * low, 2 * high, one, 0)
-        size = high - low
-        for e in range(2):
-            start_local(
-                pltpu.make_async_copy(
-                    pr.at[pl.ds(2 * low + e * size, size)],
-                    grad_out.at[pl.ds(low if e == 0 else depth - high, size)],
-                    out_sem.at[4 + 2 * r + e],
-                )
-            )
+        lax.fori_loop(0, width, one, 0)
 
     pack_part(0)
     send_part(0)
@@ -611,18 +607,19 @@
     each(0, 1, backward(3))
     go(back_halo[2])
     each(2, 8, backward(4))
-    each(1, 2, backward(3))
     each(2, 8, backward(3))
-    each(1, 2, backward(2))
-    each(2, 8, backward(2))
+    each(3, 4, backward(2))
+    each(4, 8, backward(2))
     each(4, 8, backward(1))
     hand_in(0)
-    each(2, 4, backward(1))
-    hand_in(1)
+    each(1, 2, backward(3))
+    each(1, 3, backward(2))
     arrived(back_halo[2])
     each(0, 1, backward(2))
     go(back_halo[3])
     start_local(pltpu.make_async_copy(ab.at[NT], adjoint_out.at[0, 0], out_sem.at[2]))
+    each(2, 4, backward(1))
+    hand_in(1)
     each(1, 2, backward(1))
     hand_in(2)
     arrived(back_halo[3])
@@ -641,17 +638,6 @@
         wait()
     for _, wait in due:
         wait()
-
-
-def deliver(grad, wave, adjoint, grad_out, wave_out, adjoint_out, sem):
-    copies = [pltpu.make_async_copy(grad, grad_out, sem.at[0])]
-    for e in range(2):
-        copies.append(pltpu.make_async_copy(wave.at[0, e], wave_out.at[0, e], sem.at[1 + e]))
-        copies.append(pltpu.make_async_copy(adjoint.at[0, e], adjoint_out.at[0, e], sem.at[3 + e]))
-    for copy in copies:
-        copy.start()
-    for copy in copies:
-        copy.wait()
 
 
 def shards(
@@ -675,7 +661,7 @@
     vmem = pl.BlockSpec(memory_space=pltpu.VMEM)
     padded = (depth + 2, ap + 2 * PAD, ap)
     plain = (depth, ap, ap)
-    results = pl.pallas_call(
+    return pl.pallas_call(
         kernel,
         out_shape=(
             pltpu.VMEM(kappa.shape, f32),
@@ -683,7 +669,7 @@
             pltpu.VMEM(adjoint_start.shape, f32),
         ),
         in_specs=[smem, smem, smem, any_space, any_space, any_space, any_space, vmem, vmem],
-        out_specs=(any_space, any_space, any_space),
+        out_specs=(vmem, any_space, any_space),
         scratch_shapes=[
             pltpu.VMEM((2, 2, depth, own, side), f32),
             pltpu.VMEM((7, depth, 2, own, ap), f32),
@@ -719,7 +705,7 @@
             pltpu.SemaphoreType.DMA((len(RETURNS), 7)),
             pltpu.SemaphoreType.DMA((len(RETURNS),)),
             pltpu.SemaphoreType.DMA((len(RETURNS),)),
-            pltpu.SemaphoreType.DMA((4 + 2 * len(RETURNS),)),
+            pltpu.SemaphoreType.DMA((4,)),
         ],
         compiler_params=pltpu.CompilerParams(
             collective_id=0, has_side_effects=True, vmem_limit_bytes=57 * 1024 * 1024
@@ -735,9 +721,6 @@
         jnp.transpose(receiver_cells, (2, 0, 1)),
         observed[0],
     )
-    return results
-
-
 def solution(mesh):
     in_specs = (
         P("slab", "shot", None),

time: 78 us -> 74.5 us (0.955)
  Pallas kernels: 73.9 us -> 70.1 us
    pallas_call x1, Pallas kernels: 73.9 us -> 70.1 us  [shards(): pl.pallas_call(kernel, out_shape=(pltpu.VMEM(kappa.shape, f32), pltpu.VME...]
where the time goes in v5:
time: 74.5 us; the launch traced here: 74.1 us
  Pallas kernels  70.1 us (94%)
  local copies, waits for them, and re-layouts  3.34 us (4%)
    pallas_call x1, Pallas kernels, shards(): pl.pallas_call(kernel, out_shape=(pltpu.VMEM(kappa.shape, f32), pltpu.VME...  70.1 us
    unnamed x3, local copies, waits for them, and re-layouts  3.34 us

profile of v5, /device:TPU:0, one launch (start us, length us, event | category | flops | bytes accessed | tf_op | source)
XLA Modules:
  0.0 74.1 jit_solution(6837988961004034584)
XLA Ops:
  0.6 70.1 %shard_map.112 = (f32[16,16,256]{2,1,0:T(8,128)S(1)}, f32[1,2,16,128,128]{4,3,2,1,0:T(8,128)S(1)}, f32[1,2,16,128,128]{4,3,2,1,0:T(8,128)S(1)}) custom-call(s32[2,16]{1,0:T(2,128)} %bitcast.5, f32[1,4]{1,0:T(1,128)} %wavelet.1, s32[1,3]{1,0:T(1,128)} %source.1, f32[16,16,256]{2,1,0:T(8,128)} %kappa.1, f32[16,16,256]{2,1,0:T(8,128)} %buoyancy.1, ...), custom_call_target="tpu_custom_call" | custom-call | tf_op jit(solution)/shard_map/pallas_call | solution.py:664
  70.7 0.7 copy.15
  71.4 1.3 %copy.16 = f32[1,2,16,128,128]{4,3,2,1,0:T(8,128)} copy(f32[1,2,16,128,128]{4,3,2,1,0:T(8,128)S(1)} %get-tuple-element.4) | data formatting | bytes 4194304
  72.7 1.3 %copy.17 = f32[1,2,16,128,128]{4,3,2,1,0:T(8,128)} copy(f32[1,2,16,128,128]{4,3,2,1,0:T(8,128)S(1)} %get-tuple-element.5) | data formatting | bytes 4194304

commit v6 on v5

--- a/solution.py
+++ b/solution.py
@@ -565,7 +565,6 @@
     settle(0)
     go(buoy_halo)
     pack_part(3)
-    sent_part(1)
     send_part(3)
     arrived(wave_halo[0])
     settle(1)

time: 74.5 us -> 74.5 us (level)
  no operation moved by 1% of the time
where the time goes in v6:
time: 74.5 us; the launch traced here: 74.1 us
  Pallas kernels  70.1 us (94%)
  local copies, waits for them, and re-layouts  3.34 us (4%)
    pallas_call x1, Pallas kernels, shards(): pl.pallas_call(kernel, out_shape=(pltpu.VMEM(kappa.shape, f32), pltpu.VME...  70.1 us
    unnamed x3, local copies, waits for them, and re-layouts  3.34 us

profile of v6, /device:TPU:0, one launch (start us, length us, event | category | flops | bytes accessed | tf_op | source)
XLA Modules:
  0.0 74.1 jit_solution(11342199877949474477)
XLA Ops:
  0.6 70.1 %shard_map.112 = (f32[16,16,256]{2,1,0:T(8,128)S(1)}, f32[1,2,16,128,128]{4,3,2,1,0:T(8,128)S(1)}, f32[1,2,16,128,128]{4,3,2,1,0:T(8,128)S(1)}) custom-call(s32[2,16]{1,0:T(2,128)} %bitcast.5, f32[1,4]{1,0:T(1,128)} %wavelet.1, s32[1,3]{1,0:T(1,128)} %source.1, f32[16,16,256]{2,1,0:T(8,128)} %kappa.1, f32[16,16,256]{2,1,0:T(8,128)} %buoyancy.1, ...), custom_call_target="tpu_custom_call" | custom-call | tf_op jit(solution)/shard_map/pallas_call | solution.py:663
  70.7 0.7 copy.15
  71.4 1.3 %copy.16 = f32[1,2,16,128,128]{4,3,2,1,0:T(8,128)} copy(f32[1,2,16,128,128]{4,3,2,1,0:T(8,128)S(1)} %get-tuple-element.4) | data formatting | bytes 4194304
  72.8 1.3 %copy.17 = f32[1,2,16,128,128]{4,3,2,1,0:T(8,128)} copy(f32[1,2,16,128,128]{4,3,2,1,0:T(8,128)S(1)} %get-tuple-element.5) | data formatting | bytes 4194304
